TPU v7x, 32 devices: a whole 2x2x4 slice. The times are simulated.
32 devices in a mesh: store: 8 (over z, x), tp: 4 (over y, core).
Axes of the slice: x: 2, y: 2, z: 4, core: 2. Of those that a mesh axis runs over, the one named last changes fastest.
Arguments:
- kv_store: bfloat16 [24, 2, 256, 512], P('store', None, None, 'tp'), may hold values from -6 to 6
- kv_scale: bfloat16 [24, 2, 4, 2], P('store', None, 'tp'), may hold values from 0.25 to 40
- span_home: int32 [24], replicated, may hold values from 0 to 23, as said below
- doc_ids: int32 [8, 20], P('store'), may hold values from 0 to 23, as said below
- doc_count: int32 [8], P('store'), may hold values from 6 to 20, as said below
- recompute_rows: int32 [8, 4, 128], P('store'), may hold values from 0 to 5119, as said below
- query_len: int32 [8], P('store'), may hold values from 1 to 256, as said below
- hidden: bfloat16 [8, 768, 4096], P('store', None, 'tp'), may hold values from -400 to 400
- norm_gain: bfloat16 [4096], replicated, may hold values from 0.5 to 1.5
- w_q: bfloat16 [4096, 2048], P(None, 'tp'), may hold values from -0.09375 to 0.09375
- w_kv: bfloat16 [4096, 2, 512], P(None, None, 'tp'), may hold values from -0.09375 to 0.09375
Outputs:
- attn_out: bfloat16 [8, 256, 2048], P('store', None, 'tp')
- context_kv: bfloat16 [8, 2, 5120, 512], P('store', None, None, 'tp')
Inputs may be any that keep to these rules, and one draw needn't show every extreme that they name: `span_home`: each storage position occurs once; position p lies on index p // 3 of store. `doc_ids`: the 20 ids of a request are distinct; the first doc_count are its documents; a request's ids name at most 3 spans stored on one index of store, and exactly 3 on some index. `doc_count`: some request has 20 documents. `recompute_rows`: distinct within a request and below doc_count * 256. `query_len`: some request has 256 query tokens.
All inputs are finite; a program needn't handle non-finite values.
Results may differ from a plain program's by a relative error of at most 0.015.
The roundings to bfloat16 on the way count: a program that leaves them out, or rounds other values in their place, can miss the bound.
Values may be sent and summed in bfloat16 or wider, within the bound.
A program may use at most 128 MiB of HBM per device.

v0:
```python
import jax
import jax.numpy as jnp
from jax import lax
from jax.sharding import PartitionSpec as P

SPAN = 256
SB = 128
MAXDOC = 20


rope_base = 500000.0
norm_eps = 1e-05


def rope_angles(positions, head_width):
    halfway = head_width // 2
    exponent = jnp.arange(halfway, dtype=jnp.float32) * (2.0 / head_width)
    inverse_freq = jnp.power(jnp.float32(rope_base), -exponent)
    angles = positions.astype(jnp.float32)[:, None] * inverse_freq[None, :]
    return (jnp.cos(angles), jnp.sin(angles))


def rotate_half(values, cosine, sine_part):
    halfway = values.shape[-1] // 2
    low_half = values[..., :halfway]
    high_half = values[..., halfway:]
    return jnp.concatenate(
        [low_half * cosine - high_half * sine_part, high_half * cosine + low_half * sine_part],
        axis=-1,
    )


def on_device(
    kv_store,
    kv_scale,
    span_home,
    doc_ids,
    doc_count,
    recompute_rows,
    query_len,
    hidden,
    norm_gain,
    w_q,
    w_kv,
):
    peer_count = lax.axis_size("store")
    capacity = max(2, (MAXDOC + peer_count - 1) // peer_count)
    stored = kv_store.shape[0]
    head_width = kv_store.shape[3]
    blocks = kv_scale.shape[3]
    doc_list = doc_ids[0]
    doc_total = doc_count[0]
    span_index = jnp.arange(span_home.shape[0], dtype=jnp.int32)
    position = jnp.sum(
        jnp.where(doc_list[:, None] == span_index[None, :], span_home[None, :], 0), axis=1
    )
    owner_dev = position // stored
    slot_index = position % stored
    slot_range = jnp.arange(MAXDOC)
    before = slot_range[:, None] > slot_range[None, :]
    same_owner = owner_dev[:, None] == owner_dev[None, :]
    copy_rank = jnp.sum(jnp.where(before & same_owner, 1, 0), axis=1)
    mailbox = owner_dev * capacity + copy_rank
    placed = mailbox[:, None] == jnp.arange(peer_count * capacity)[None, :]
    wanted = jnp.sum(jnp.where(placed, slot_index[:, None], 0), axis=0).reshape(
        peer_count, capacity
    )
    asked = lax.all_to_all(wanted, "store", split_axis=0, concat_axis=0, tiled=True)
    asked_flat = asked.reshape(peer_count * capacity)
    send_codes = jnp.take(kv_store, asked_flat, axis=0).reshape(
        peer_count, capacity, 2, SPAN, head_width
    )
    send_scales = jnp.take(kv_scale, asked_flat, axis=0).reshape(peer_count, capacity, 2, blocks)
    got_codes, got_scales = (
        lax.all_to_all(send_codes, "store", split_axis=0, concat_axis=0, tiled=True),
        lax.all_to_all(send_scales, "store", split_axis=0, concat_axis=0, tiled=True),
    )
    codes = jnp.take(got_codes.reshape(peer_count * capacity, 2, SPAN, head_width), mailbox, axis=0)
    scales = jnp.take(got_scales.reshape(peer_count * capacity, 2, blocks), mailbox, axis=0)
    block_scale = jnp.repeat(scales.astype(jnp.float32), SB, axis=2)
    dequant = codes.astype(jnp.float32) * block_scale[..., None]
    shift_cos, shift_sin = rope_angles(jnp.arange(MAXDOC, dtype=jnp.int32) * SPAN, head_width)
    cached_keys = rotate_half(dequant[:, 0], shift_cos[:, None, :], shift_sin[:, None, :])
    context_max = MAXDOC * SPAN
    live_rows = jnp.arange(context_max) < doc_total * SPAN
    cached_keys = jnp.where(
        live_rows[:, None], cached_keys.reshape(context_max, head_width), 0.0
    ).astype(jnp.bfloat16)
    cached_values = jnp.where(
        live_rows[:, None], dequant[:, 1].reshape(context_max, head_width), 0.0
    ).astype(jnp.bfloat16)
    layer_input = lax.all_gather(hidden, "tp", axis=2, tiled=True)[0]
    features = layer_input.astype(jnp.float32)
    inverse_rms = lax.rsqrt(jnp.mean(features * features, axis=-1, keepdims=True) + norm_eps)
    normed = (features * inverse_rms * norm_gain.astype(jnp.float32)).astype(jnp.bfloat16)
    recompute_total = recompute_rows.shape[1] * recompute_rows.shape[2]
    query_rows = layer_input.shape[0] - recompute_total
    query_heads = w_q.shape[1] // head_width
    query_proj = jnp.dot(normed[recompute_total:], w_q, preferred_element_type=jnp.float32)
    kv_proj = jnp.dot(
        normed, w_kv.reshape(w_kv.shape[0], 2 * head_width), preferred_element_type=jnp.float32
    )
    kv_proj = kv_proj.reshape(-1, 2, head_width)
    flat_pos = recompute_rows[0].reshape(recompute_total)
    query_pos = doc_total * SPAN + jnp.arange(query_rows, dtype=jnp.int32)
    row_cos, row_sin = rope_angles(jnp.concatenate([flat_pos, query_pos]), head_width)
    new_keys = rotate_half(kv_proj[:, 0], row_cos, row_sin).astype(jnp.bfloat16)
    new_values = kv_proj[:, 1].astype(jnp.bfloat16)
    queries = rotate_half(
        query_proj.reshape(query_rows, query_heads, head_width),
        row_cos[recompute_total:, None, :],
        row_sin[recompute_total:, None, :],
    ).astype(jnp.bfloat16)
    patched_keys = cached_keys.at[flat_pos].set(new_keys[:recompute_total])
    patched_values = cached_values.at[flat_pos].set(new_values[:recompute_total])
    all_keys = jnp.concatenate([patched_keys, new_keys[recompute_total:]], axis=0)
    all_values = jnp.concatenate([patched_values, new_values[recompute_total:]], axis=0)
    query_matrix = jnp.transpose(queries, (1, 0, 2)).reshape(query_heads * query_rows, head_width)
    scores = lax.dot_general(
        query_matrix, all_keys, (((1,), (1,)), ((), ())), preferred_element_type=jnp.float32
    ) * head_width ** (-0.5)
    query_index = jnp.arange(query_heads * query_rows) % query_rows
    key_index = jnp.arange(context_max + query_rows)
    allowed = jnp.where(
        key_index[None, :] < context_max,
        (key_index < doc_total * SPAN)[None, :],
        key_index[None, :] - context_max <= query_index[:, None],
    )
    scores = jnp.where(allowed, scores, -jnp.inf)
    top_score = jnp.max(scores, axis=-1, keepdims=True)
    exp_terms = jnp.where(allowed, jnp.exp(scores - top_score), 0.0)
    weights = (exp_terms / jnp.sum(exp_terms, axis=-1, keepdims=True)).astype(jnp.bfloat16)
    mixed_rows = jnp.dot(weights, all_values, preferred_element_type=jnp.float32)
    mixed_rows = jnp.where((query_index < query_len[0])[:, None], mixed_rows, 0.0)
    attention = jnp.transpose(mixed_rows.reshape(query_heads, query_rows, head_width), (1, 0, 2))
    attention = attention.reshape(1, query_rows, query_heads * head_width).astype(jnp.bfloat16)
    context_kv = jnp.stack([patched_keys, patched_values], axis=0)[None]
    return (attention, context_kv)


def solution(mesh):
    placed = (
        P("store", None, None, "tp"),
        P("store", None, "tp", None),
        P(),
        P("store", None),
        P("store"),
        P("store", None, None),
        P("store"),
        P("store", None, "tp"),
        P(),
        P(None, "tp"),
        P(None, None, "tp"),
    )
    return jax.shard_map(
        on_device,
        mesh=mesh,
        in_specs=placed,
        out_specs=(P("store", None, "tp"), P("store", None, None, "tp")),
        check_vma=False,
    )
```

profile of v0, /device:TPU:0, one launch (start us, length us, event | category | flops | bytes accessed | tf_op | source)
XLA Modules:
  0.0 187.9 jit_solution(15837238221573593146)
XLA Ops:
  11.9 7.3 %all-to-all-start = ((s32[8,1,3]{2,1,0:T(1,128)}), s32[8,1,3]{2,1,0:T(1,128)S(1)}, u32[]{:S(2)}, u32[]{:S(2)}) async-start(s32[8,1,3]{2,1,0:T(1,128)} %bitcast.7), calls=%async_computation | async-start | bytes 8192 | tf_op jit(solution)/shard_map/all_to_all | solution.py:68
  19.9 5.6 %all-to-all-done = s32[8,1,3]{2,1,0:T(1,128)S(1)} async-done(((s32[8,1,3]{2,1,0:T(1,128)}), s32[8,1,3]{2,1,0:T(1,128)S(1)}, u32[]{:S(2)}, u32[]{:S(2)}) %all-to-all-start) | async-done | bytes 128 | tf_op jit(solution)/shard_map/all_to_all | solution.py:68
  28.4 3.3 %all-to-all-start.2 = ((bf16[8,3,2,2]{1,3,2,0:T(2,128)(2,1)}), bf16[8,3,2,2]{1,3,2,0:T(2,128)(2,1)S(1)}, u32[]{:S(2)}, u32[]{:S(2)}) async-start(bf16[8,3,2,2]{1,3,2,0:T(2,128)(2,1)} %copy.68), calls=%async_computation.2 | async-start | bytes 16384 | tf_op jit(solution)/shard_map/all_to_all | solution.py:76
  32.9 2.1 %broadcast_select_fusion = bf16[8,3,2,256,128]{4,3,2,1,0:T(8,128)(2,1)} fusion(bf16[8,3,2,256,128]{4,3,2,1,0:T(8,128)(2,1)S(1)} %bitcast.84, pred[8,3]{1,0:T(8,128)(4,1)S(1)} %copy.64), kind=kLoop, calls=%fused_computation.25 | loop fusion | flops 1572864 | bytes 6291480 | tf_op jit(solution)/shard_map/jit(_take)/select_n | solution.py:70
  35.0 3.2 %all-to-all-done.2 = bf16[8,3,2,2]{1,3,2,0:T(2,128)(2,1)S(1)} async-done(((bf16[8,3,2,2]{1,3,2,0:T(2,128)(2,1)}), bf16[8,3,2,2]{1,3,2,0:T(2,128)(2,1)S(1)}, u32[]{:S(2)}, u32[]{:S(2)}) %all-to-all-start.2) | async-done | bytes 224 | tf_op jit(solution)/shard_map/all_to_all | solution.py:76
  38.2 3.6 %all-to-all-start.1 = ((bf16[8,3,2,256,128]{4,3,2,1,0:T(8,128)(2,1)}), bf16[8,3,2,256,128]{4,3,2,1,0:T(8,128)(2,1)S(1)}, u32[]{:S(2)}, u32[]{:S(2)}) async-start(bf16[8,3,2,256,128]{4,3,2,1,0:T(8,128)(2,1)} %broadcast_select_fusion), calls=%async_computation.1 | async-start | bytes 6291456 | tf_op jit(solution)/shard_map/all_to_all | solution.py:75
  41.8 3.2 %copy.88 = bf16[512,8,2,128]{3,1,2,0:T(8,128)(2,1)} copy(bf16[512,8,2,128]{3,2,1,0:T(2,128)(2,1)} %bitcast.89) | data formatting | bytes 4194304
  45.1 4.2 %copy.71 = bf16[256,4096]{1,0:T(8,128)(2,1)} copy(bf16[256,4096]{0,1:T(8,128)(2,1)} %bitcast.88) | data formatting | bytes 4194304 | tf_op jit(solution)/shard_map/dot_general | solution.py:100
  56.1 54.1 %all-to-all-done.1 = bf16[8,3,2,256,128]{4,3,2,1,0:T(8,128)(2,1)S(1)} async-done(((bf16[8,3,2,256,128]{4,3,2,1,0:T(8,128)(2,1)}), bf16[8,3,2,256,128]{4,3,2,1,0:T(8,128)(2,1)S(1)}, u32[]{:S(2)}, u32[]{:S(2)}) %all-to-all-start.1) | async-done | bytes 3145760 | tf_op jit(solution)/shard_map/all_to_all | solution.py:75
  110.2 2.5 %gather_fusion.1 = bf16[20,2,256,128]{3,2,1,0:T(8,128)(2,1)} fusion(bf16[24,2,256,128]{3,2,1,0:T(8,128)(2,1)S(1)} %bitcast.85, s32[1024]{0:T(1024)S(1)} %pad_clamp_fusion), kind=kCustom, calls=%fused_computation.1 | custom fusion | bytes 5242960 | tf_op jit(solution)/shard_map/jit(_take)/gather | solution.py:78
  112.7 3.5 %convert_multiply_fusion.1 = f32[20,2,256,128]{3,2,1,0:T(8,128)S(1)} fusion(f32[20,2,256]{2,1,0:T(2,128)S(1)} %mul.241, bf16[20,2,256,128]{3,2,1,0:T(8,128)(2,1)} %gather_fusion.1, pred[20]{0:T(512)(128)(4,1)S(1)} %copy-done.14), kind=kLoop, calls=%fused_computation.21 | loop fusion | flops 3932160 | bytes 7905300 | tf_op jit(solution)/shard_map/mul | solution.py:81
  118.4 2.9 %fusion.12 = (bf16[5120,128]{1,0:T(8,128)(2,1)S(1)}, bf16[5120,128]{1,0:T(8,128)(2,1)S(1)}) fusion(bf16[20,256,128]{2,1,0:T(8,128)(2,1)S(1)} %pad_maximum_fusion, pred[5120]{0:T(1024)(128)(4,1)S(1)} %iota_compare_fusion.2, bf16[20,1,256,128]{3,2,1,0:T(8,128)(2,1)S(1)} %slice.98), kind=kLoop, calls=%fused_computation.32 | loop fusion | flops 1310720 | bytes 5248000 | tf_op jit(solution)/shard_map/convert_element_type | solution.py:88
  121.3 4.2 %multiply_reduce_fusion = f32[768]{0:T(1024)S(1)} fusion(bf16[1,768,4096]{2,1,0:T(8,128)(2,1)} %all-gather.2.cloned.1.call-done), kind=kLoop, calls=%fused_computation.15 | loop fusion | flops 9436416 | bytes 6294528 | tf_op jit(solution)/shard_map/reduce_sum | solution.py:94
  125.9 3.7 %fusion.44 = (bf16[768,2,128]{0,2,1:T(8,128)(2,1)S(1)}, f32[768,2,128]{0,2,1:T(8,128)S(1)}) fusion(bf16[2,128,4096]{2,1,0:T(8,128)(2,1)} %bitcast.90, bf16[1,768,4096]{2,1,0:T(8,128)(2,1)S(1)} %copy-done.2, f32[4096]{0:T(1024)S(1)} %copy-done.11, f32[768]{0:T(1024)S(1)} %add_rsqrt_fusion), kind=kOutput, calls=%fused_computation.112 | convolution fusion | flops 1623392256 | bytes 9587712 | tf_op jit(solution)/shard_map/dot_general | solution.py:100
  129.7 1.6 subtract_convert_fusion.1
  132.7 4.5 %convert_bitcast_fusion = f32[768,4096]{1,0:T(8,128)S(1)} fusion(bf16[1,768,4096]{2,1,0:T(8,128)(2,1)} %all-gather.2.cloned.1.call-done), kind=kLoop, calls=%fused_computation.12 | loop fusion | flops 3145728 | bytes 18874368 | tf_op jit(solution)/shard_map/convert_element_type | solution.py:93
  137.3 4.3 %fusion.13 = f32[256,512]{1,0:T(8,128)} fusion(bf16[4096,512]{1,0:T(8,128)(2,1)} %param.20, f32[768,4096]{1,0:T(8,128)S(1)} %convert_bitcast_fusion, f32[4096]{0:T(1024)S(1)} %copy-done.11, f32[256]{0:T(256)S(1)} %slice.85), kind=kOutput, calls=%fused_computation.35 | convolution fusion | flops 1076887552 | bytes 8930304 | tf_op jit(solution)/shard_map/dot_general | solution.py:99
  146.2 1.4 subtract_convert_fusion
  148.5 2.5 %scatter_fusion.1 = bf16[5120,128]{1,0:T(8,128)(2,1)S(1)} fusion(bf16[5120,128]{1,0:T(8,128)(2,1)S(1)} %get-tuple-element.15, s32[512]{0:T(512)S(1)} %bitcast.95, bf16[512,128]{1,0:T(8,128)(2,1)S(1)} %copy-done.3), kind=kCustom, calls=%fused_computation.5 | custom fusion | bytes 395264 | tf_op jit(solution)/shard_map/scatter | solution.py:115
  151.0 2.7 %scatter_fusion = bf16[5120,128]{1,0:T(8,128)(2,1)S(1)} fusion(bf16[5120,128]{1,0:T(8,128)(2,1)S(1)} %get-tuple-element.14, s32[512]{0:T(512)S(1)} %bitcast.96, bf16[512,128]{1,0:T(8,128)(2,1)S(1)} %copy.72), kind=kCustom, calls=%fused_computation.4 | custom fusion | bytes 395264 | tf_op jit(solution)/shard_map/scatter | solution.py:114
  153.8 5.7 %fusion = (f32[1024]{0:T(1024)S(1)}, f32[1024,5376]{1,0:T(8,128)S(1)}) fusion(s32[5376]{0:T(1024)S(1)} %copy-done.5, s32[1024]{0:T(1024)S(1)} %copy-done.10, pred[5376]{0:T(1024)(128)(4,1)S(1)} %get-tuple-element.25, pred[5376]{0:T(1024)(128)(4,1)S(1)} %copy-done.7, bf16[1024,128]{1,0:T(8,128)(2,1)S(1)} %bitcast.91, bf16[256,128]{1,0:T(8,128)(2,1)S(1)} %copy.73, ...), kind=kOutput, calls=%fused_computation.10 | convolution fusion | flops 1439562752 | bytes 23698944 | tf_op jit(solution)/shard_map/dot_general | solution.py:119
  159.4 10.4 %fusion.42 = f32[1024]{0:T(1024)S(1)} fusion(f32[1024]{0:T(1024)S(1)} %get-tuple-element.23, f32[1024,5376]{1,0:T(8,128)S(1)} %get-tuple-element.24, s32[1024]{0:T(1024)S(1)} %copy-done.10, s32[5376]{0:T(1024)S(1)} %copy-done.5, pred[5376]{0:T(1024)(128)(4,1)S(1)} %get-tuple-element.25, pred[5376]{0:T(1024)(128)(4,1)S(1)} %copy-done.7), kind=kLoop, calls=%fused_computation.110 | loop fusion | flops 38534144 | bytes 22064640 | tf_op jit(solution)/shard_map/reduce_sum | solution.py:132
  169.9 8.4 %fusion.27 = bf16[1024,128]{1,0:T(8,128)(2,1)S(1)} fusion(bf16[256,128]{1,0:T(8,128)(2,1)S(1)} %copy-done.6, bf16[5120,128]{1,0:T(8,128)(2,1)S(1)} %scatter_fusion.1, f32[1024]{0:T(1024)S(1)} %fusion.42, pred[1024]{0:T(1024)(128)(4,1)S(1)} %copy-done.22, f32[1024,5376]{1,0:T(8,128)S(1)} %get-tuple-element.24, f32[1024]{0:T(1024)S(1)} %get-tuple-element.23, ...), kind=kOutput, calls=%fused_computation.47 | convolution fusion | flops 1456340992 | bytes 23704064 | tf_op jit(solution)/shard_map/dot_general | solution.py:133
  179.4 1.7 maximum_bitcast_fusion
  (112 shorter events, 25.5 us)
Async XLA Ops:
  7.2 24.6 %copy-start = (bf16[3,2,256,128]{3,2,1,0:T(8,128)(2,1)S(1)}, bf16[3,2,256,128]{3,2,1,0:T(8,128)(2,1)}, u32[]{:S(2)}) copy-start(bf16[3,2,256,128]{3,2,1,0:T(8,128)(2,1)} %param.11) | copy-start | bytes 1179652
  7.2 114.1 %all-gather.2.cloned.1.call-start = ((), (), s32[]{:S(2)}) async-start(), calls=%async_computation.3 | async-start | bytes 7864320 | tf_op jit(solution)/shard_map/all_gather | solution.py:92
  11.9 13.6 %all-to-all-start = ((s32[8,1,3]{2,1,0:T(1,128)}), s32[8,1,3]{2,1,0:T(1,128)S(1)}, u32[]{:S(2)}, u32[]{:S(2)}) async-start(s32[8,1,3]{2,1,0:T(1,128)} %bitcast.7), calls=%async_computation | async-start | bytes 8192 | tf_op jit(solution)/shard_map/all_to_all | solution.py:68
  28.4 9.8 %all-to-all-start.2 = ((bf16[8,3,2,2]{1,3,2,0:T(2,128)(2,1)}), bf16[8,3,2,2]{1,3,2,0:T(2,128)(2,1)S(1)}, u32[]{:S(2)}, u32[]{:S(2)}) async-start(bf16[8,3,2,2]{1,3,2,0:T(2,128)(2,1)} %copy.68), calls=%async_computation.2 | async-start | bytes 16384 | tf_op jit(solution)/shard_map/all_to_all | solution.py:76
  38.2 72.0 %all-to-all-start.1 = ((bf16[8,3,2,256,128]{4,3,2,1,0:T(8,128)(2,1)}), bf16[8,3,2,256,128]{4,3,2,1,0:T(8,128)(2,1)S(1)}, u32[]{:S(2)}, u32[]{:S(2)}) async-start(bf16[8,3,2,256,128]{4,3,2,1,0:T(8,128)(2,1)} %broadcast_select_fusion), calls=%async_computation.1 | async-start | bytes 6291456 | tf_op jit(solution)/shard_map/all_to_all | solution.py:75
  45.0 4.2 %copy-start.12 = (bf16[4096]{0:T(1024)(128)(2,1)S(1)}, bf16[4096]{0:T(1024)(128)(2,1)}, u32[]{:S(2)}) copy-start(bf16[4096]{0:T(1024)(128)(2,1)} %param.19) | copy-start | bytes 24580
  45.0 7.4 %copy-start.18 = (s32[20]{0:T(128)S(1)}, s32[20]{0:T(128)}, u32[]{:S(2)}) copy-start(s32[20]{0:T(128)} %copy-done.17) | copy-start | bytes 244
  45.0 7.4 %copy-start.19 = (s32[20]{0:T(128)S(1)}, s32[20]{0:T(128)}, u32[]{:S(2)}) copy-start(s32[20]{0:T(128)} %get-tuple-element.5) | copy-start | bytes 244
  45.0 7.4 %copy-start.21 = (s32[20]{0:T(128)S(1)}, s32[20]{0:T(128)}, u32[]{:S(2)}) copy-start(s32[20]{0:T(128)} %copy-done.20) | copy-start | bytes 244
  45.0 7.4 %copy-start.13 = (s32[1,4,128]{2,1,0:T(4,128)S(1)}, s32[1,4,128]{2,1,0:T(4,128)}, u32[]{:S(2)}) copy-start(s32[1,4,128]{2,1,0:T(4,128)} %param.16) | copy-start | bytes 6148
  45.1 10.7 %copy-start.14 = (pred[20]{0:T(512)(128)(4,1)S(1)}, pred[20]{0:T(512)(128)(4,1)}, u32[]{:S(2)}) copy-start(pred[20]{0:T(512)(128)(4,1)} %get-tuple-element.2) | copy-start | bytes 64
  51.2 3.7 %copy-start.15 = (f32[64]{0:T(128)}, f32[64]{0:T(128)S(1)}, u32[]{:S(2)}) copy-start(f32[64]{0:T(128)S(1)} %negate_power_fusion) | copy-start | bytes 772
  118.4 7.2 %copy-start.11 = (f32[4096]{0:T(1024)S(1)}, f32[4096]{0:T(1024)}, u32[]{:S(2)}) copy-start(f32[4096]{0:T(1024)} %convert_element_type.81) | copy-start | bytes 49156
  121.3 4.6 %copy-start.2 = (bf16[1,768,4096]{2,1,0:T(8,128)(2,1)S(1)}, bf16[1,768,4096]{2,1,0:T(8,128)(2,1)}, u32[]{:S(2)}) copy-start(bf16[1,768,4096]{2,1,0:T(8,128)(2,1)} %all-gather.2.cloned.1.call-done) | copy-start | bytes 18874372
  125.9 3.7 %copy-start.9 = (f32[768]{0:T(1024)S(1)}, f32[768]{0:T(1024)}, u32[]{:S(2)}) copy-start(f32[768]{0:T(1024)} %add_convert_fusion.2) | copy-start | bytes 9220
  125.9 3.8 %copy-start.16 = (f32[64]{0:T(128)S(1)}, f32[64]{0:T(128)}, u32[]{:S(2)}) copy-start(f32[64]{0:T(128)} %copy-done.15) | copy-start | bytes 772
  142.8 5.7 %copy-start.8 = (s32[512,1]{0,1:T(1,128)S(1)}, s32[512,1]{0,1:T(1,128)}, u32[]{:S(2)}) copy-start(s32[512,1]{0,1:T(1,128)} %compare_select_fusion.1) | copy-start | bytes 6148
  144.0 4.4 %copy-start.3 = (bf16[512,128]{1,0:T(8,128)(2,1)S(1)}, bf16[512,128]{1,0:T(8,128)(2,1)}, u32[]{:S(2)}) copy-start(bf16[512,128]{1,0:T(8,128)(2,1)} %copy.74) | copy-start | bytes 393220
  146.2 7.5 %copy-start.5 = (s32[5376]{0:T(1024)S(1)}, s32[5376]{0:T(1024)}, u32[]{:S(2)}) copy-start(s32[5376]{0:T(1024)} %iota_add_fusion) | copy-start | bytes 64516
  146.2 7.5 %copy-start.7 = (pred[5376]{0:T(1024)(128)(4,1)S(1)}, pred[5376]{0:T(1024)(128)(4,1)}, u32[]{:S(2)}) copy-start(pred[5376]{0:T(1024)(128)(4,1)} %get-tuple-element.26) | copy-start | bytes 16132
  146.2 7.5 %copy-start.10 = (s32[1024]{0:T(1024)S(1)}, s32[1024]{0:T(1024)}, u32[]{:S(2)}) copy-start(s32[1024]{0:T(1024)} %add_select_fusion) | copy-start | bytes 12292
  148.4 5.3 %copy-start.4 = (bf16[256,4,128]{2,0,1:T(8,128)(2,1)S(1)}, bf16[256,4,128]{2,0,1:T(8,128)(2,1)}, u32[]{:S(2)}) copy-start(bf16[256,4,128]{2,0,1:T(8,128)(2,1)} %pad_maximum_fusion.1) | copy-start | bytes 786436
  159.4 10.4 %copy-start.6 = (bf16[256,128]{1,0:T(8,128)(2,1)S(1)}, bf16[256,128]{1,0:T(8,128)(2,1)}, u32[]{:S(2)}) copy-start(bf16[256,128]{1,0:T(8,128)(2,1)} %copy.75) | copy-start | bytes 196612
  159.4 10.4 %copy-start.22 = (pred[1024]{0:T(1024)(128)(4,1)S(1)}, pred[1024]{0:T(1024)(128)(4,1)}, u32[]{:S(2)}) copy-start(pred[1024]{0:T(1024)(128)(4,1)} %broadcast_compare_fusion) | copy-start | bytes 3076
  (3 other events, 3.8 us)
Sparse Core Ops, SparseCore 0:
  9.6 49.0 all-gather.1
where the time goes:
time: 189 us; the launch traced here: 188 us
  waiting for transfers between devices  63.6 us (34%)
  other arithmetic  42.2 us (22%)
  local copies, waits for them, and re-layouts  30 us (16%)
  matrix products  22 us (12%)
  between operations  15.8 us (8%)
  starting transfers between devices  14.3 us (8%)
    all_to_all x1, waiting for transfers between devices, on_device(): lax.all_to_all(send_codes, 'store', split_axis=0, concat_axis=0, tiled=True)  54.1 us
    reduce_sum x1, other arithmetic, on_device(): jnp.sum(exp_terms, axis=-1, keepdims=True)  10.4 us
    dot_general x1, matrix products, on_device(): jnp.dot(weights, all_values, preferred_element_type=jnp.float32)  8.44 us
    all_to_all x1, starting transfers between devices, on_device(): lax.all_to_all(wanted, 'store', split_axis=0, concat_axis=0, tiled=True)  7.25 us
    dot_general x1, matrix products, on_device(): lax.dot_general(query_matrix, all_keys, (((1,), (1,)), ((), ())), preferr...  5.66 us
    all_to_all x1, waiting for transfers between devices, on_device(): lax.all_to_all(wanted, 'store', split_axis=0, concat_axis=0, tiled=True)  5.6 us
    unnamed x48, local copies, waits for them, and re-layouts  5.5 us
    convert_element_type x1, other arithmetic, on_device(): features = layer_input.astype(jnp.float32)  4.51 us
  transfers between devices with their start and end apart: 4, of which 3 were waited for; matrix products, arithmetic and copies ran while one was open for 18% of the time, Pallas kernels for 0%

commit v1 on v0

v1 whole, which is shorter than its diff:
```python
import functools

import jax
import jax.numpy as jnp
import numpy as np
from jax import lax
from jax.experimental import pallas as pl
from jax.experimental.pallas import tpu as pltpu
from jax.sharding import PartitionSpec as P

SPAN = 256
SB = 128
MAXDOC = 20
HEAD = 128
HALF = HEAD // 2
CHUNK = 128
SCALE_ROWS = 16
rope_base = 500000.0
norm_eps = 1e-05
f32, bf16 = jnp.float32, jnp.bfloat16
MESH = pl.DeviceIdType.MESH
ANY = pl.BlockSpec(memory_space=pl.ANY)
VMEM = pl.BlockSpec(memory_space=pltpu.VMEM)
SMEM = pl.BlockSpec(memory_space=pltpu.SMEM)


def inverse_freq():
    half = np.power(rope_base, -np.arange(HALF) * (2.0 / HEAD)).astype(np.float32)
    return np.concatenate([half, half])


def rotate(values, cosine, signed_sine):
    return values * cosine + pltpu.roll(values, HALF, 1) * signed_sine


def gather_kernel(
    hidden, codes, scales, w_q, w_kv, gain, angles,
    q_out, k_out, v_out, codes_out, scales_out,
    hid, wq, wkv_raw, wkv, wide,
    local_sem, hid_send, hid_recv, up_send, down_send, x_send, z_recv, x_recv,
):
    s = lax.axis_index("store")
    t = lax.axis_index("tp")
    z, x = s // 2, s % 2
    y, c = t // 2, t % 2
    last = 3
    across = (1 - y) * 2 + c
    sibling = y * 2 + (1 - c)
    diagonal = (1 - y) * 2 + (1 - c)
    x_peer = z * 2 + (1 - x)

    barrier = pltpu.get_barrier_semaphore()

    def greet(axis, index):
        pl.semaphore_signal(barrier, inc=1, device_id={axis: index}, device_id_type=MESH)

    greet("tp", across)
    greet("tp", sibling)
    greet("store", x_peer)
    pl.when(z > 0)(lambda: greet("store", s - 2))
    pl.when(z < last)(lambda: greet("store", s + 2))
    pl.semaphore_wait(barrier, 3 + jnp.where(z > 0, 1, 0) + jnp.where(z < last, 1, 0))

    def span_copies(own, owner_z, column, send, recv, target):
        slot = owner_z * 2 + column
        pairs = ((codes if own else codes_out.at[slot], codes_out.at[slot], 0),
                 (scales if own else scales_out.at[slot], scales_out.at[slot], 1))
        return [
            pltpu.make_async_remote_copy(
                src_ref=src, dst_ref=dst, send_sem=send.at[owner_z, i], recv_sem=recv.at[owner_z, i],
                device_id={"store": target}, device_id_type=MESH,
            )
            for src, dst, i in pairs
        ]

    def start_all(copies):
        for copy in copies:
            copy.start()

    def up(own, owner_z):
        return span_copies(own, owner_z, x, up_send, z_recv, s + 2)

    def down(own, owner_z):
        return span_copies(own, owner_z, x, down_send, z_recv, s - 2)

    def over(own, owner_z):
        return span_copies(own, owner_z, x, x_send, x_recv, x_peer)

    def hidden_copy(kind, chunk):
        rows = pl.ds(chunk * CHUNK, CHUNK)
        slot = across if kind == 2 else t
        return pltpu.make_async_remote_copy(
            src_ref=hid.at[slot, rows] if kind == 2 else hidden.at[rows],
            dst_ref=hid.at[slot, rows],
            send_sem=hid_send.at[kind, chunk], recv_sem=hid_recv.at[kind, chunk],
            device_id={"tp": across if kind == 0 else sibling}, device_id_type=MESH,
        )

    def hidden_arrival(kind, chunk):
        rows = pl.ds(chunk * CHUNK, CHUNK)
        slot = (across, sibling, diagonal)[kind]
        pltpu.make_async_remote_copy(
            src_ref=hidden.at[rows], dst_ref=hid.at[slot, rows],
            send_sem=hid_send.at[kind, chunk], recv_sem=hid_recv.at[kind, chunk],
            device_id={"tp": across if kind == 0 else sibling}, device_id_type=MESH,
        ).wait_recv()

    chunks = hidden.shape[0] // CHUNK
    query_chunks = q_out.shape[1] // CHUNK
    order = list(range(chunks - query_chunks, chunks)) + list(range(chunks - query_chunks))

    pl.when(z < last)(lambda: start_all(up(True, z)))
    pl.when(z > 0)(lambda: start_all(down(True, z)))
    start_all(over(True, z))
    for chunk in order:
        hidden_copy(0, chunk).start()
    for chunk in order:
        hidden_copy(1, chunk).start()
    local = [
        pltpu.make_async_copy(w_kv, wkv_raw, local_sem.at[0]),
        pltpu.make_async_copy(w_q, wq, local_sem.at[1]),
        pltpu.make_async_copy(hidden, hid.at[t], local_sem.at[2]),
        pltpu.make_async_copy(codes, codes_out.at[s], local_sem.at[3]),
        pltpu.make_async_copy(scales, scales_out.at[s], local_sem.at[4]),
    ]
    start_all(local)
    local[0].wait()
    block = wide.shape[0]

    def split_pairs(i, carry):
        wide[...] = wkv_raw[pl.ds(pl.multiple_of(i * block, block), block), :].astype(f32)
        rows = pl.ds(pl.multiple_of(i * (block // 2), block // 2), block // 2)
        wkv[rows, 0:HEAD] = wide[pl.ds(0, block // 2, stride=2), :].astype(bf16)
        wkv[rows, HEAD:2 * HEAD] = wide[pl.ds(1, block // 2, stride=2), :].astype(bf16)
        return carry

    lax.fori_loop(0, wkv_raw.shape[0] // block, split_pairs, 0)
    for copy in local[1:]:
        copy.wait()

    parts, _, width = hid.shape

    def project(chunk):
        rows = pl.ds(chunk * CHUNK, CHUNK)
        squares = jnp.zeros((CHUNK, 1), f32)
        for part in range(parts):
            values = hid[part, rows, :].astype(f32)
            squares = squares + jnp.sum(values * values, axis=1, keepdims=True)
        inverse_rms = lax.rsqrt(squares * (1.0 / (parts * width)) + norm_eps)
        kv = jnp.zeros((CHUNK, 2 * HEAD), f32)
        is_query = chunk >= chunks - query_chunks
        q = jnp.zeros((CHUNK, wq.shape[1]), f32)
        for part in range(parts):
            columns = pl.ds(part * width, width)
            normed = (hid[part, rows, :].astype(f32) * inverse_rms * gain[:, columns]).astype(bf16)
            kv = kv + jnp.dot(normed, wkv[columns, :], preferred_element_type=f32)
            if is_query:
                q = q + jnp.dot(normed, wq[columns, :], preferred_element_type=f32)
        angle = angles[rows, :]
        cosine = jnp.cos(angle)
        lane = lax.broadcasted_iota(jnp.int32, angle.shape, 1)
        sine = jnp.sin(angle)
        sine = jnp.where(lane < HALF, -sine, sine)
        k_out[rows, :] = rotate(kv[:, :HEAD], cosine, sine)
        v_out[rows, :] = kv[:, HEAD:]
        if is_query:
            q_rows = pl.ds((chunk - (chunks - query_chunks)) * CHUNK, CHUNK)
            for g in range(q_out.shape[0]):
                q_out[g, q_rows, :] = rotate(q[:, g * HEAD:(g + 1) * HEAD], cosine, sine).astype(bf16)

    def span_step(k):
        @pl.when(z >= k)
        def _():
            for copy in up(False, z - k):
                copy.wait_recv()
            pl.when(z < last)(lambda: start_all(up(False, z - k)))
            start_all(over(False, z - k))

        @pl.when(z + k <= last)
        def _():
            for copy in down(False, z + k):
                copy.wait_recv()
            pl.when(z > 0)(lambda: start_all(down(False, z + k)))
            start_all(over(False, z + k))

    hooks = {0: 1, 2: 2, 3: 3}
    for i in range(chunks + 1):
        if i < chunks:
            hidden_arrival(0, order[i])
            hidden_copy(2, order[i]).start()
        if i in hooks:
            span_step(hooks[i])
        if i > 0:
            hidden_arrival(1, order[i - 1])
            hidden_arrival(2, order[i - 1])
            project(order[i - 1])

    for owner in range(4):
        for copy in span_copies(False, owner, 1 - x, x_send, x_recv, x_peer):
            copy.wait_recv()
    for chunk in range(chunks):
        for kind in range(3):
            hidden_copy(kind, chunk).wait_send()
    for owner in range(4):
        for copy in over(False, owner):
            copy.wait_send()

        @pl.when(jnp.logical_and(z < last, owner <= z))
        def _():
            for copy in up(False, owner):
                copy.wait_send()

        @pl.when(jnp.logical_and(z > 0, owner >= z))
        def _():
            for copy in down(False, owner):
                copy.wait_send()


def gather_and_project(peers, tp, hidden, codes, scales, w_q, w_kv, gain, angles):
    rows, width = hidden.shape
    features = w_q.shape[0]
    heads = w_q.shape[1] // HEAD
    chunks = rows // CHUNK
    return pl.pallas_call(
        gather_kernel,
        out_shape=(
            jax.ShapeDtypeStruct((heads, SPAN, HEAD), bf16),
            jax.ShapeDtypeStruct((rows, HEAD), f32),
            jax.ShapeDtypeStruct((rows, HEAD), f32),
            jax.ShapeDtypeStruct((peers,) + codes.shape, bf16),
            jax.ShapeDtypeStruct((peers,) + scales.shape, bf16),
        ),
        in_specs=[ANY, ANY, ANY, ANY, ANY, VMEM, VMEM],
        out_specs=(VMEM, VMEM, VMEM, ANY, ANY),
        scratch_shapes=[
            pltpu.VMEM((tp, rows, width), bf16),
            pltpu.VMEM((features, w_q.shape[1]), bf16),
            pltpu.VMEM((2 * features, HEAD), bf16),
            pltpu.VMEM((features, 2 * HEAD), bf16),
            pltpu.VMEM((512, HEAD), f32),
            pltpu.SemaphoreType.DMA((5,)),
            pltpu.SemaphoreType.DMA((3, chunks)),
            pltpu.SemaphoreType.DMA((3, chunks)),
            pltpu.SemaphoreType.DMA((4, 2)),
            pltpu.SemaphoreType.DMA((4, 2)),
            pltpu.SemaphoreType.DMA((4, 2)),
            pltpu.SemaphoreType.DMA((4, 2)),
            pltpu.SemaphoreType.DMA((4, 2)),
        ],
        compiler_params=pltpu.CompilerParams(
            collective_id=0, has_side_effects=True, vmem_limit_bytes=48 * 2**20
        ),
        name="gather_project",
    )(hidden, codes, scales, w_q, w_kv, gain, angles)


def plain_gather_and_project(hidden, codes, scales, w_q, w_kv, gain, angles):
    rows = hidden.shape[0]
    heads = w_q.shape[1] // HEAD
    all_codes = lax.all_gather(codes, "store", axis=0)
    all_scales = lax.all_gather(scales, "store", axis=0)
    features = lax.all_gather(hidden, "tp", axis=1, tiled=True).astype(f32)
    inverse_rms = lax.rsqrt(jnp.mean(features * features, axis=-1, keepdims=True) + norm_eps)
    normed = (features * inverse_rms * gain).astype(bf16)
    cosine, sine = jnp.cos(angles), jnp.sin(angles)
    sine = jnp.where(jnp.arange(HEAD)[None, :] < HALF, -sine, sine)
    kv = jnp.dot(normed, w_kv.reshape(-1, 2 * HEAD), preferred_element_type=f32)
    q = jnp.dot(normed[rows - SPAN:], w_q, preferred_element_type=f32)
    q = jnp.transpose(q.reshape(SPAN, heads, HEAD), (1, 0, 2))

    def turn(values, cosine, sine):
        return values * cosine + jnp.roll(values, HALF, axis=-1) * sine

    new_keys = turn(kv[:, :HEAD], cosine, sine)
    q = turn(q, cosine[rows - SPAN:], sine[rows - SPAN:]).astype(bf16)
    return q, new_keys, kv[:, HEAD:], all_codes, all_scales


def attend_kernel(
    stored, home, ids, count, recompute, query_len, codes, scales, doc_cos, doc_sin, q, new_k, new_v,
    out, context,
    fetched, scale_rows, key_rows, value_rows, keys, values, scores, top, total, mixed, fetch_sem, out_sem,
):
    docs = count[0]
    recompute_total = recompute.shape[0]
    context_max = MAXDOC * SPAN
    heads = q.shape[0]

    def fetch(j):
        position = home[ids[0, j]]
        return pltpu.make_async_copy(codes.at[position], fetched.at[j], fetch_sem.at[j])

    lax.fori_loop(0, docs, lambda j, n: (fetch(j).start(), n)[1], 0)
    scale_rows[...] = scales[...].astype(f32)

    def dequantise(j, carry):
        base = pl.multiple_of(j * SPAN, SPAN)

        @pl.when(j < docs)
        def _():
            fetch(j).wait()
            position = home[ids[0, j]]
            first = (position // stored) * SCALE_ROWS + (position % stored) * 4
            cosine, sine = doc_cos[pl.ds(j, 1), :], doc_sin[pl.ds(j, 1), :]
            for b in range(SPAN // SB):
                rows = pl.ds(base + b * SB, SB)
                k = fetched[j, 0, b * SB:(b + 1) * SB, :].astype(f32) * scale_rows[pl.ds(first + b, 1), :]
                key_rows[rows, :] = rotate(k, cosine, sine)
                v = fetched[j, 1, b * SB:(b + 1) * SB, :].astype(f32) * scale_rows[pl.ds(first + 2 + b, 1), :]
                value_rows[rows, :] = v

        @pl.when(j >= docs)
        def _():
            key_rows[pl.ds(base, SPAN), :] = jnp.zeros((SPAN, HEAD), f32)
            value_rows[pl.ds(base, SPAN), :] = jnp.zeros((SPAN, HEAD), f32)

        return carry

    lax.fori_loop(0, MAXDOC, dequantise, 0)

    def patch(i, carry):
        for u in range(8):
            source = i * 8 + u
            row = recompute[source]
            key_rows[pl.ds(row, 1), :] = new_k[pl.ds(source, 1), :]
            value_rows[pl.ds(row, 1), :] = new_v[pl.ds(source, 1), :]
        return carry

    lax.fori_loop(0, recompute_total // 8, patch, 0)

    def narrow(j, carry):
        rows = pl.ds(pl.multiple_of(j * SPAN, SPAN), SPAN)
        keys[rows, :] = key_rows[rows, :].astype(bf16)
        values[rows, :] = value_rows[rows, :].astype(bf16)
        return carry

    lax.fori_loop(0, MAXDOC, narrow, 0)
    keys[context_max:context_max + SPAN, :] = new_k[recompute_total:, :].astype(bf16)
    values[context_max:context_max + SPAN, :] = new_v[recompute_total:, :].astype(bf16)
    writes = [
        pltpu.make_async_copy(keys.at[0:context_max], context.at[0], out_sem.at[0]),
        pltpu.make_async_copy(values.at[0:context_max], context.at[1], out_sem.at[1]),
    ]
    for copy in writes:
        copy.start()

    def score(g, rows):
        return lax.dot_general(q[g], keys[rows, :], (((1,), (1,)), ((), ())), preferred_element_type=f32)

    own_rows = pl.ds(context_max, SPAN)
    query_index = lax.broadcasted_iota(jnp.int32, (SPAN, SPAN), 0)
    key_index = lax.broadcasted_iota(jnp.int32, (SPAN, SPAN), 1)
    for g in range(heads):
        own = jnp.where(key_index <= query_index, score(g, own_rows), -1e30)
        scores[MAXDOC, g] = own
        top[g] = jnp.maximum(own[:, :HEAD], own[:, HEAD:])

    def first_pass(j, carry):
        rows = pl.ds(pl.multiple_of(j * SPAN, SPAN), SPAN)
        for g in range(heads):
            block = score(g, rows)
            scores[j, g] = block
            top[g] = jnp.maximum(top[g], jnp.maximum(block[:, :HEAD], block[:, HEAD:]))
        return carry

    lax.fori_loop(0, docs, first_pass, 0)
    for g in range(heads):
        top[g] = jnp.broadcast_to(jnp.max(top[g], axis=1, keepdims=True), (SPAN, HEAD))
        total[g] = jnp.zeros((SPAN, HEAD), f32)
        mixed[g] = jnp.zeros((SPAN, HEAD), f32)

    def weigh(slot, rows):
        for g in range(heads):
            peak = top[g]
            low = jnp.exp((scores[slot, g, :, :HEAD] - peak) * HEAD ** (-0.5))
            high = jnp.exp((scores[slot, g, :, HEAD:] - peak) * HEAD ** (-0.5))
            total[g] += low + high
            weights = jnp.concatenate([low.astype(bf16), high.astype(bf16)], axis=1)
            mixed[g] += jnp.dot(weights, values[rows, :], preferred_element_type=f32)

    def second_pass(j, carry):
        weigh(j, pl.ds(pl.multiple_of(j * SPAN, SPAN), SPAN))
        return carry

    lax.fori_loop(0, docs, second_pass, 0)
    weigh(MAXDOC, own_rows)
    live = lax.broadcasted_iota(jnp.int32, (SPAN, HEAD), 0) < query_len[0]
    for g in range(heads):
        result = mixed[g] / jnp.sum(total[g], axis=1, keepdims=True)
        out[:, g * HEAD:(g + 1) * HEAD] = jnp.where(live, result, 0.0).astype(bf16)
    for copy in writes:
        copy.wait()


def attend(stored, home, ids, count, recompute, query_len, codes, scales, q, new_k, new_v):
    context_max = MAXDOC * SPAN
    heads = q.shape[0]
    freq = inverse_freq()
    angle = ((np.arange(24) * SPAN).astype(np.float32)[:, None] * freq[None, :]).astype(np.float64)
    sign = np.where(np.arange(HEAD) < HALF, -1.0, 1.0)
    doc_cos = np.cos(angle).astype(np.float32)
    doc_sin = (np.sin(angle) * sign).astype(np.float32)
    return pl.pallas_call(
        functools.partial(attend_kernel, stored),
        out_shape=(
            jax.ShapeDtypeStruct((SPAN, heads * HEAD), bf16),
            jax.ShapeDtypeStruct((2, context_max, HEAD), bf16),
        ),
        in_specs=[SMEM] * 5 + [ANY] + [VMEM] * 6,
        out_specs=(VMEM, ANY),
        scratch_shapes=[
            pltpu.VMEM((MAXDOC, 2, SPAN, HEAD), bf16),
            pltpu.VMEM(scales.shape, f32),
            pltpu.VMEM((context_max, HEAD), f32),
            pltpu.VMEM((context_max, HEAD), f32),
            pltpu.VMEM((context_max + SPAN, HEAD), bf16),
            pltpu.VMEM((context_max + SPAN, HEAD), bf16),
            pltpu.VMEM((MAXDOC + 1, heads, SPAN, SPAN), f32),
            pltpu.VMEM((heads, SPAN, HEAD), f32),
            pltpu.VMEM((heads, SPAN, HEAD), f32),
            pltpu.VMEM((heads, SPAN, HEAD), f32),
            pltpu.SemaphoreType.DMA((MAXDOC,)),
            pltpu.SemaphoreType.DMA((2,)),
        ],
        compiler_params=pltpu.CompilerParams(vmem_limit_bytes=48 * 2**20),
        name="patch_attend",
    )(home, ids, count, recompute, query_len, codes, scales, doc_cos, doc_sin, q, new_k, new_v)


def on_device(
    kv_store, kv_scale, span_home, doc_ids, doc_count, recompute_rows, query_len, hidden, norm_gain, w_q, w_kv,
):
    peers, tp = lax.axis_size("store"), lax.axis_size("tp")
    stored = kv_store.shape[0]
    scales = jnp.broadcast_to(kv_scale.reshape(stored * 4, 1), (stored * 4, HEAD))
    scales = jnp.pad(scales, ((0, SCALE_ROWS - stored * 4), (0, 0)))
    flat = recompute_rows.reshape(-1)
    row_pos = jnp.concatenate([flat, doc_count[0] * SPAN + jnp.arange(SPAN, dtype=jnp.int32)])
    angles = row_pos.astype(f32)[:, None] * inverse_freq()[None, :]
    gain = norm_gain.astype(f32).reshape(1, -1)
    pairs = w_kv.reshape(-1, HEAD)
    if (peers, tp) == (8, 4):
        gathered = gather_and_project(peers, tp, hidden[0], kv_store, scales, w_q, pairs, gain, angles)
    else:
        gathered = plain_gather_and_project(hidden[0], kv_store, scales, w_q, pairs, gain, angles)
    q, new_k, new_v, codes, all_scales = gathered
    attention, context = attend(
        stored, span_home, doc_ids, doc_count, flat, query_len,
        codes.reshape((peers * stored,) + kv_store.shape[1:]), all_scales.reshape(-1, HEAD), q, new_k, new_v,
    )
    return attention[None], context[None]


def solution(mesh):
    placed = (
        P("store", None, None, "tp"),
        P("store", None, "tp", None),
        P(),
        P("store", None),
        P("store"),
        P("store", None, None),
        P("store"),
        P("store", None, "tp"),
        P(),
        P(None, "tp"),
        P(None, None, "tp"),
    )
    return jax.shard_map(
        on_device,
        mesh=mesh,
        in_specs=placed,
        out_specs=(P("store", None, "tp"), P("store", None, None, "tp")),
        check_vma=False,
    )
```

time: 189 us -> 75.1 us (0.40)
  the two profiles are of different devices: /device:TPU:0 before, /device:TPU:25 now
where the time goes in v1:
time: 75.1 us; the launch traced here: 74.7 us
  Pallas kernels  63.6 us (85%)
  local copies, waits for them, and re-layouts  6.85 us (9%)
  other arithmetic  2.21 us (3%)
  between operations  2.02 us (3%)
    pallas_call x1, Pallas kernels, gather_and_project(): pl.pallas_call(gather_kernel, out_shape=(jax.ShapeDtypeStruct((heads, SPA...  40.7 us
    pallas_call x1, Pallas kernels, attend(): pl.pallas_call(functools.partial(attend_kernel, stored), out_shape=(jax.S...  22.8 us
    unnamed x19, local copies, waits for them, and re-layouts  6.68 us

profile of v1, /device:TPU:25, one launch (start us, length us, event | category | flops | bytes accessed | tf_op | source)
XLA Modules:
  0.0 74.7 jit_solution(6322375868547953032)
XLA Ops:
  1.9 0.8 %copy.17 = bf16[3,2,1,2]{3,1,0,2:T(2,128)(2,1)S(1)} copy(bf16[3,2,1,2]{0,3,2,1:T(2,128)(2,1)} %param.15) | data formatting | bytes 48 | tf_op args[1]
  2.7 0.1 broadcast_in_dim.12
  2.8 0.7 add_convert_fusion
  3.5 0.1 pad.7.scales
  3.6 0.7 reshape.46
  4.3 0.8 %broadcast_multiply_fusion.angles = f32[768,128]{1,0:T(8,128)S(1)} fusion(f32[128]{0:T(128)} %constant.24, f32[768]{0:T(1024)S(1)} %add_convert_fusion), kind=kLoop, calls=%fused_computation | loop fusion | flops 98304 | bytes 396800 | tf_op jit(solution)/shard_map/mul | solution.py:439
  5.1 0.0 copy-start.1
  5.1 1.6 %copy-done.1 = bf16[4096,2,128]{2,1,0:T(2,128)(2,1)S(1)} copy-done((bf16[4096,2,128]{2,1,0:T(2,128)(2,1)S(1)}, bf16[4096,2,128]{2,1,0:T(2,128)(2,1)}, u32[]{:S(2)}) %copy-start.1) | copy-done | bytes 2097176
  6.7 0.0 copy-start.2
  6.7 1.4 %copy-done.2 = bf16[1,768,1024]{2,1,0:T(8,128)(2,1)S(1)} copy-done((bf16[1,768,1024]{2,1,0:T(8,128)(2,1)S(1)}, bf16[1,768,1024]{2,1,0:T(8,128)(2,1)}, u32[]{:S(2)}) %copy-start.2) | copy-done | bytes 1572888
  8.1 0.0 copy-start.3
  8.1 1.0 %copy-done.3 = bf16[3,2,256,128]{3,2,1,0:T(8,128)(2,1)S(1)} copy-done((bf16[3,2,256,128]{3,2,1,0:T(8,128)(2,1)S(1)}, bf16[3,2,256,128]{3,2,1,0:T(8,128)(2,1)}, u32[]{:S(2)}) %copy-start.3) | copy-done | bytes 393240
  9.1 0.0 copy-start.4
  9.1 0.0 copy-start.5
  9.1 0.0 copy-start.8
  9.1 40.7 %gather_project.1 = (bf16[4,256,128]{2,1,0:T(8,128)(2,1)S(1)}, f32[768,128]{1,0:T(8,128)S(1)}, f32[768,128]{1,0:T(8,128)S(1)}, bf16[8,3,2,256,128]{4,3,2,1,0:T(8,128)(2,1)}, bf16[8,16,128]{2,1,0:T(8,128)(2,1)S(1)}) custom-call(bf16[768,1024]{1,0:T(8,128)(2,1)S(1)} %bitcast.13, bf16[3,2,256,128]{3,2,1,0:T(8,128)(2,1)S(1)} %copy-done.3, ...), custom_call_target="tpu_custom_call" | custom-call | tf_op jit(solution)/shard_map/gather_project/pallas_call | solution.py:224
  49.9 0.0 copy-done.4
  49.9 0.0 copy-done.5
  49.9 0.0 copy-done.6
  49.9 0.0 copy-done.7
  49.9 0.0 copy-done.8
  49.9 0.0 copy-start
  49.9 1.9 %copy-done = bf16[8,3,2,256,128]{4,3,2,1,0:T(8,128)(2,1)S(1)} copy-done((bf16[8,3,2,256,128]{4,3,2,1,0:T(8,128)(2,1)S(1)}, bf16[8,3,2,256,128]{4,3,2,1,0:T(8,128)(2,1)}, u32[]{:S(2)}) %copy-start) | copy-done | bytes 3145752
  51.8 22.8 %patch_attend.1 = (bf16[256,512]{1,0:T(8,128)(2,1)}, bf16[2,5120,128]{2,1,0:T(8,128)(2,1)}) custom-call(s32[24]{0:T(128)S(1)} %copy-done.7, s32[1,20]{1,0:T(1,128)S(1)} %copy-done.8, s32[1]{0:T(128)S(6)} %copy.18.count, s32[512]{0:T(512)S(1)} %bitcast.17, s32[1]{0:T(128)S(6)} %copy.19.query_len, bf16[24,2,256,128]{3,2,1,0:T(8,128)(2,1)S(1)} %bitcast.11, ...), custom_call_target="tpu_custom_call" | custom-call | tf_op jit(solution)/shard_map/patch_attend/pallas_call | solution.py:403
  (4 shorter events, 0.0 us)
Async XLA Ops:
  5.1 1.6 %copy-start.1 = (bf16[4096,2,128]{2,1,0:T(2,128)(2,1)S(1)}, bf16[4096,2,128]{2,1,0:T(2,128)(2,1)}, u32[]{:S(2)}) copy-start(bf16[4096,2,128]{2,1,0:T(2,128)(2,1)} %param.24) | copy-start | bytes 6291460
  6.7 1.4 %copy-start.2 = (bf16[1,768,1024]{2,1,0:T(8,128)(2,1)S(1)}, bf16[1,768,1024]{2,1,0:T(8,128)(2,1)}, u32[]{:S(2)}) copy-start(bf16[1,768,1024]{2,1,0:T(8,128)(2,1)} %param.21) | copy-start | bytes 4718596
  8.1 1.0 %copy-start.3 = (bf16[3,2,256,128]{3,2,1,0:T(8,128)(2,1)S(1)}, bf16[3,2,256,128]{3,2,1,0:T(8,128)(2,1)}, u32[]{:S(2)}) copy-start(bf16[3,2,256,128]{3,2,1,0:T(8,128)(2,1)} %codes.1) | copy-start | bytes 1179652
  9.1 40.8 %copy-start.4 = (f32[24,128]{1,0:T(8,128)S(1)}, f32[24,128]{1,0:T(8,128)}, u32[]{:S(2)}) copy-start(f32[24,128]{1,0:T(8,128)} %constant.14.clone.doc_sin) | copy-start | bytes 36868
  9.1 40.8 %copy-start.5 = (f32[24,128]{1,0:T(8,128)S(1)}, f32[24,128]{1,0:T(8,128)}, u32[]{:S(2)}) copy-start(f32[24,128]{1,0:T(8,128)} %constant.13.clone.doc_cos) | copy-start | bytes 36868
  9.1 40.8 %copy-start.6 = (s32[1,4,128]{2,1,0:T(4,128)S(1)}, s32[1,4,128]{2,1,0:T(4,128)}, u32[]{:S(2)}) copy-start(s32[1,4,128]{2,1,0:T(4,128)} %param.19) | copy-start | bytes 6148
  9.1 40.8 %copy-start.7 = (s32[24]{0:T(128)S(1)}, s32[24]{0:T(128)}, u32[]{:S(2)}) copy-start(s32[24]{0:T(128)} %home.1) | copy-start | bytes 292
  9.1 40.8 %copy-start.8 = (s32[1,20]{1,0:T(1,128)S(1)}, s32[1,20]{1,0:T(1,128)}, u32[]{:S(2)}) copy-start(s32[1,20]{1,0:T(1,128)} %ids.1) | copy-start | bytes 244
  49.9 1.9 %copy-start = (bf16[8,3,2,256,128]{4,3,2,1,0:T(8,128)(2,1)S(1)}, bf16[8,3,2,256,128]{4,3,2,1,0:T(8,128)(2,1)}, u32[]{:S(2)}) copy-start(bf16[8,3,2,256,128]{4,3,2,1,0:T(8,128)(2,1)} %get-tuple-element.9) | copy-start | bytes 9437188

commit v2 on v1

--- a/solution.py
+++ b/solution.py
@@ -17,6 +17,8 @@
 SCALE_ROWS = 16
 rope_base = 500000.0
 norm_eps = 1e-05
+MASKED = -1e30
+LOG2E = 1.4426950408889634
 f32, bf16 = jnp.float32, jnp.bfloat16
 MESH = pl.DeviceIdType.MESH
 ANY = pl.BlockSpec(memory_space=pl.ANY)
@@ -33,11 +35,17 @@
     return values * cosine + pltpu.roll(values, HALF, 1) * signed_sine
 
 
-def gather_kernel(
-    hidden, codes, scales, w_q, w_kv, gain, angles,
-    q_out, k_out, v_out, codes_out, scales_out,
-    hid, wq, wkv_raw, wkv, wide,
-    local_sem, hid_send, hid_recv, up_send, down_send, x_send, z_recv, x_recv,
+def doc_tables(rows):
+    angle = ((np.arange(rows) * SPAN).astype(np.float32)[:, None] * inverse_freq()[None, :]).astype(np.float64)
+    sign = np.where(np.arange(HEAD) < HALF, -1.0, 1.0)
+    return np.cos(angle).astype(np.float32), (np.sin(angle) * sign).astype(np.float32)
+
+
+def stream_kernel(
+    home, ids, count, query_len, hidden, codes, scales, w_q, w_kv, gain, recompute, freq, doc_cos, doc_sin,
+    attn_out, k_out, v_out, cached_out,
+    hid, wq, wkv_raw, wkv, wide, codes_all, scales_own, scales_all, cached, queries, scores, top, total, mixed, hidden_rows,
+    local_sem, cached_sem, hid_send, hid_recv, up_send, down_send, x_send, z_recv, x_recv,
 ):
     s = lax.axis_index("store")
     t = lax.axis_index("tp")
@@ -59,12 +67,33 @@
     greet("store", x_peer)
     pl.when(z > 0)(lambda: greet("store", s - 2))
     pl.when(z < last)(lambda: greet("store", s + 2))
+
+    local = [
+        pltpu.make_async_copy(w_kv, wkv_raw, local_sem.at[0]),
+        pltpu.make_async_copy(w_q, wq, local_sem.at[1]),
+        pltpu.make_async_copy(hidden, hid.at[t], local_sem.at[2]),
+        pltpu.make_async_copy(codes, codes_all.at[s], local_sem.at[3]),
+    ]
+
+    def start_all(copies):
+        for copy in copies:
+            copy.start()
+
+    start_all(local)
+    stored, blocks = codes.shape[0], SPAN // SB
+    scales_own[...] = jnp.zeros(scales_own.shape, f32)
+    for i in range(stored):
+        for part in range(2):
+            pair = scales[i, part].astype(f32)
+            for b in range(blocks):
+                row = (i * 2 + part) * blocks + b
+                scales_own[row:row + 1, :] = jnp.broadcast_to(pair[:, b:b + 1], (1, HEAD))
     pl.semaphore_wait(barrier, 3 + jnp.where(z > 0, 1, 0) + jnp.where(z < last, 1, 0))
 
     def span_copies(own, owner_z, column, send, recv, target):
         slot = owner_z * 2 + column
-        pairs = ((codes if own else codes_out.at[slot], codes_out.at[slot], 0),
-                 (scales if own else scales_out.at[slot], scales_out.at[slot], 1))
+        pairs = ((codes if own else codes_all.at[slot], codes_all.at[slot], 0),
+                 (scales_own if own else scales_all.at[slot], scales_all.at[slot], 1))
         return [
             pltpu.make_async_remote_copy(
                 src_ref=src, dst_ref=dst, send_sem=send.at[owner_z, i], recv_sem=recv.at[owner_z, i],
@@ -72,10 +101,6 @@
             )
             for src, dst, i in pairs
         ]
-
-    def start_all(copies):
-        for copy in copies:
-            copy.start()
 
     def up(own, owner_z):
         return span_copies(own, owner_z, x, up_send, z_recv, s + 2)
@@ -106,24 +131,36 @@
         ).wait_recv()
 
     chunks = hidden.shape[0] // CHUNK
-    query_chunks = q_out.shape[1] // CHUNK
-    order = list(range(chunks - query_chunks, chunks)) + list(range(chunks - query_chunks))
-
+    query_chunks = SPAN // CHUNK
+    first_query = chunks - query_chunks
+    order = list(range(first_query, chunks)) + list(range(first_query))
+
+    start_all(over(True, z))
     pl.when(z < last)(lambda: start_all(up(True, z)))
     pl.when(z > 0)(lambda: start_all(down(True, z)))
-    start_all(over(True, z))
     for chunk in order:
         hidden_copy(0, chunk).start()
     for chunk in order:
         hidden_copy(1, chunk).start()
-    local = [
-        pltpu.make_async_copy(w_kv, wkv_raw, local_sem.at[0]),
-        pltpu.make_async_copy(w_q, wq, local_sem.at[1]),
-        pltpu.make_async_copy(hidden, hid.at[t], local_sem.at[2]),
-        pltpu.make_async_copy(codes, codes_out.at[s], local_sem.at[3]),
-        pltpu.make_async_copy(scales, scales_out.at[s], local_sem.at[4]),
-    ]
-    start_all(local)
+
+    docs = count[0]
+    positions = [home[ids[0, j]] for j in range(MAXDOC)]
+    table_rows = hidden_rows.shape[0]
+    hits = jnp.zeros((table_rows, SPAN), f32)
+    for r in range(recompute.shape[0]):
+        row = recompute[r:r + 1, :]
+        doc_match = lax.broadcasted_iota(jnp.int32, (table_rows, CHUNK), 0) == (row >> 8)
+        row_match = lax.broadcasted_iota(jnp.int32, (SPAN, CHUNK), 0) == (row & 255)
+        hits = hits + lax.dot_general(
+            jnp.where(doc_match, 1.0, 0.0).astype(bf16), jnp.where(row_match, 1.0, 0.0).astype(bf16),
+            (((1,), (1,)), ((), ())), preferred_element_type=f32,
+        )
+    dead = lax.broadcasted_iota(jnp.int32, (table_rows, SPAN), 0) >= docs
+    hidden_rows[...] = jnp.where(jnp.logical_or(dead, hits > 0.5), MASKED, 0.0)
+    top[...] = jnp.full(top.shape, MASKED, f32)
+    total[...] = jnp.zeros(total.shape, f32)
+    mixed[...] = jnp.zeros(mixed.shape, f32)
+
     local[0].wait()
     block = wide.shape[0]
 
@@ -139,8 +176,22 @@
         copy.wait()
 
     parts, _, width = hid.shape
+    heads = wq.shape[1] // HEAD
+    own_slot = cached.shape[0] - 1
+
+    def row_angles(chunk):
+        if chunk >= first_query:
+            offset = docs * SPAN + (chunk - first_query) * CHUNK
+            place = lax.broadcasted_iota(jnp.int32, (CHUNK, HEAD), 0) + offset
+            return place.astype(f32) * freq[...]
+        row = jnp.broadcast_to(recompute[chunk:chunk + 1, :].astype(f32), (CHUNK, CHUNK))
+        down_rows = lax.broadcasted_iota(jnp.int32, (CHUNK, CHUNK), 0)
+        diagonal_entry = down_rows == lax.broadcasted_iota(jnp.int32, (CHUNK, CHUNK), 1)
+        return jnp.sum(jnp.where(diagonal_entry, row, 0.0), axis=1, keepdims=True) * freq[...]
 
     def project(chunk):
+        hidden_arrival(1, chunk)
+        hidden_arrival(2, chunk)
         rows = pl.ds(chunk * CHUNK, CHUNK)
         squares = jnp.zeros((CHUNK, 1), f32)
         for part in range(parts):
@@ -148,7 +199,7 @@
             squares = squares + jnp.sum(values * values, axis=1, keepdims=True)
         inverse_rms = lax.rsqrt(squares * (1.0 / (parts * width)) + norm_eps)
         kv = jnp.zeros((CHUNK, 2 * HEAD), f32)
-        is_query = chunk >= chunks - query_chunks
+        is_query = chunk >= first_query
         q = jnp.zeros((CHUNK, wq.shape[1]), f32)
         for part in range(parts):
             columns = pl.ds(part * width, width)
@@ -156,48 +207,151 @@
             kv = kv + jnp.dot(normed, wkv[columns, :], preferred_element_type=f32)
             if is_query:
                 q = q + jnp.dot(normed, wq[columns, :], preferred_element_type=f32)
-        angle = angles[rows, :]
-        cosine = jnp.cos(angle)
-        lane = lax.broadcasted_iota(jnp.int32, angle.shape, 1)
-        sine = jnp.sin(angle)
-        sine = jnp.where(lane < HALF, -sine, sine)
-        k_out[rows, :] = rotate(kv[:, :HEAD], cosine, sine)
-        v_out[rows, :] = kv[:, HEAD:]
+        angle = row_angles(chunk)
+        cosine, sine = jnp.cos(angle), jnp.sin(angle)
+        sine = jnp.where(lax.broadcasted_iota(jnp.int32, angle.shape, 1) < HALF, -sine, sine)
+        new_key = rotate(kv[:, :HEAD], cosine, sine)
+        per_span = SPAN // CHUNK
+        place = pl.ds(chunk % per_span * CHUNK, CHUNK)
+        cached[own_slot, chunk // per_span, 0, place, :] = new_key.astype(bf16)
+        cached[own_slot, chunk // per_span, 1, place, :] = kv[:, HEAD:].astype(bf16)
         if is_query:
-            q_rows = pl.ds((chunk - (chunks - query_chunks)) * CHUNK, CHUNK)
-            for g in range(q_out.shape[0]):
-                q_out[g, q_rows, :] = rotate(q[:, g * HEAD:(g + 1) * HEAD], cosine, sine).astype(bf16)
+            for g in range(heads):
+                q_rows = pl.ds(g * SPAN + (chunk - first_query) * CHUNK, CHUNK)
+                queries[q_rows, :] = rotate(q[:, g * HEAD:(g + 1) * HEAD], cosine, sine).astype(bf16)
+        else:
+            k_out[rows, :] = new_key
+            v_out[rows, :] = kv[:, HEAD:]
+
+    exponent = HEAD ** (-0.5) * LOG2E
+    query_block = scores.shape[1]
+
+    def attend_group(slot, bias, causal):
+        def some_queries(n, carry):
+            rows = pl.ds(pl.multiple_of(n * query_block, query_block), query_block)
+            q = queries[rows, :]
+            before = top[rows, :]
+            peak = before
+            for i in range(stored):
+                part = lax.dot_general(
+                    q, cached[slot, i, 0], (((1,), (1,)), ((), ())), preferred_element_type=f32
+                )
+                if bias is not None:
+                    part = part + bias[i]
+                elif causal and i == stored - 1:
+                    query_index = lax.broadcasted_iota(jnp.int32, (query_block, SPAN), 0) & (SPAN - 1)
+                    key_index = lax.broadcasted_iota(jnp.int32, (query_block, SPAN), 1)
+                    part = jnp.where(key_index <= query_index, part, MASKED)
+                scores[i] = part
+                peak = jnp.maximum(peak, jnp.maximum(part[:, :HEAD], part[:, HEAD:]))
+            peak = jnp.broadcast_to(jnp.max(peak, axis=1, keepdims=True), (query_block, HEAD))
+            top[rows, :] = peak
+            fade = jnp.exp2((before - peak) * exponent)
+            sums = total[rows, :] * fade
+            gained = jnp.zeros((query_block, HEAD), f32)
+            for i in range(stored):
+                low = jnp.exp2((scores[i, :, :HEAD] - peak) * exponent)
+                high = jnp.exp2((scores[i, :, HEAD:] - peak) * exponent)
+                sums = sums + (low + high)
+                weights = jnp.concatenate([low.astype(bf16), high.astype(bf16)], axis=1)
+                gained = gained + jnp.dot(weights, cached[slot, i, 1], preferred_element_type=f32)
+            total[rows, :] = sums
+            mixed[rows, :] = mixed[rows, :] * fade + gained
+            return carry
+
+        lax.fori_loop(0, queries.shape[0] // query_block, some_queries, 0)
+
+    def keep_cached(slot):
+        return pltpu.make_async_copy(cached.at[slot], cached_out.at[slot], cached_sem.at[slot])
+
+    def span_group(slot):
+        bias = []
+        for i in range(stored):
+            position = slot * stored + i
+            doc = table_rows - 1
+            for j in range(MAXDOC):
+                doc = doc + jnp.where(positions[j] == position, j - (table_rows - 1), 0)
+            doc = jnp.clip(doc, 0, table_rows - 1)
+            cosine, sine = doc_cos[pl.ds(doc, 1), :], doc_sin[pl.ds(doc, 1), :]
+            bias.append(hidden_rows[pl.ds(doc, 1), :])
+            for b in range(blocks):
+                rows = slice(b * SB, (b + 1) * SB)
+                first = i * 2 * blocks + b
+                k = codes_all[slot, i, 0, rows, :].astype(f32) * scales_all[slot, first:first + 1, :]
+                cached[slot, i, 0, rows, :] = rotate(k, cosine, sine).astype(bf16)
+                first = first + blocks
+                v = codes_all[slot, i, 1, rows, :].astype(f32) * scales_all[slot, first:first + 1, :]
+                cached[slot, i, 1, rows, :] = v.astype(bf16)
+        keep_cached(slot).start()
+        attend_group(slot, bias, False)
 
     def span_step(k):
         @pl.when(z >= k)
         def _():
             for copy in up(False, z - k):
                 copy.wait_recv()
+            start_all(over(False, z - k))
             pl.when(z < last)(lambda: start_all(up(False, z - k)))
-            start_all(over(False, z - k))
 
         @pl.when(z + k <= last)
         def _():
             for copy in down(False, z + k):
                 copy.wait_recv()
+            start_all(over(False, z + k))
             pl.when(z > 0)(lambda: start_all(down(False, z + k)))
-            start_all(over(False, z + k))
-
-    hooks = {0: 1, 2: 2, 3: 3}
-    for i in range(chunks + 1):
-        if i < chunks:
-            hidden_arrival(0, order[i])
-            hidden_copy(2, order[i]).start()
-        if i in hooks:
-            span_step(hooks[i])
-        if i > 0:
-            hidden_arrival(1, order[i - 1])
-            hidden_arrival(2, order[i - 1])
-            project(order[i - 1])
-
-    for owner in range(4):
-        for copy in span_copies(False, owner, 1 - x, x_send, x_recv, x_peer):
+
+    folded = jnp.where(z < 2, z, last - z)
+
+    def near(k):
+        owner = jnp.where(folded == 0, k, (1, 0, 2, 3)[k])
+        return jnp.where(z < 2, owner, last - owner)
+
+    def same_column(k):
+        span_group(near(k) * 2 + x)
+
+    def other_column(k):
+        for copy in span_copies(False, near(k), 1 - x, x_send, x_recv, x_peer):
             copy.wait_recv()
+        span_group(near(k) * 2 + 1 - x)
+
+    def relay(i):
+        hidden_arrival(0, order[i])
+        hidden_copy(2, order[i]).start()
+
+    relay(0)
+    scales_all[s] = scales_own[...]
+    project(order[0])
+    span_step(1)
+    relay(1)
+    project(order[1])
+    same_column(0)
+    relay(2)
+    span_step(2)
+    other_column(0)
+    project(order[2])
+    same_column(1)
+    relay(3)
+    span_step(3)
+    other_column(1)
+    project(order[3])
+    relay(4)
+    same_column(2)
+    same_column(3)
+    project(order[4])
+    other_column(2)
+    relay(5)
+    project(order[5])
+    attend_group(own_slot, None, True)
+    other_column(3)
+
+    live = lax.broadcasted_iota(jnp.int32, (SPAN, HEAD), 0) < query_len[0]
+    for g in range(heads):
+        rows = pl.ds(g * SPAN, SPAN)
+        result = mixed[rows, :] / jnp.sum(total[rows, :], axis=1, keepdims=True)
+        attn_out[:, g * HEAD:(g + 1) * HEAD] = jnp.where(live, result, 0.0).astype(bf16)
+
+    for slot in range(own_slot):
+        keep_cached(slot).wait()
     for chunk in range(chunks):
         for kind in range(3):
             hidden_copy(kind, chunk).wait_send()
@@ -216,42 +370,140 @@
                 copy.wait_send()
 
 
-def gather_and_project(peers, tp, hidden, codes, scales, w_q, w_kv, gain, angles):
+def stream(peers, tp, home, ids, count, query_len, hidden, codes, scales, w_q, w_kv, gain, recompute):
     rows, width = hidden.shape
     features = w_q.shape[0]
     heads = w_q.shape[1] // HEAD
     chunks = rows // CHUNK
+    table_rows = 32
+    doc_cos, doc_sin = doc_tables(table_rows)
+    fresh = rows - SPAN
+    dma = pltpu.SemaphoreType.DMA
     return pl.pallas_call(
-        gather_kernel,
+        stream_kernel,
         out_shape=(
-            jax.ShapeDtypeStruct((heads, SPAN, HEAD), bf16),
-            jax.ShapeDtypeStruct((rows, HEAD), f32),
-            jax.ShapeDtypeStruct((rows, HEAD), f32),
+            jax.ShapeDtypeStruct((SPAN, heads * HEAD), bf16),
+            jax.ShapeDtypeStruct((fresh, HEAD), f32),
+            jax.ShapeDtypeStruct((fresh, HEAD), f32),
             jax.ShapeDtypeStruct((peers,) + codes.shape, bf16),
-            jax.ShapeDtypeStruct((peers,) + scales.shape, bf16),
         ),
-        in_specs=[ANY, ANY, ANY, ANY, ANY, VMEM, VMEM],
-        out_specs=(VMEM, VMEM, VMEM, ANY, ANY),
+        in_specs=[SMEM] * 4 + [ANY, ANY, VMEM, ANY, ANY] + [VMEM] * 5,
+        out_specs=(VMEM, VMEM, VMEM, ANY),
         scratch_shapes=[
             pltpu.VMEM((tp, rows, width), bf16),
             pltpu.VMEM((features, w_q.shape[1]), bf16),
             pltpu.VMEM((2 * features, HEAD), bf16),
             pltpu.VMEM((features, 2 * HEAD), bf16),
             pltpu.VMEM((512, HEAD), f32),
-            pltpu.SemaphoreType.DMA((5,)),
-            pltpu.SemaphoreType.DMA((3, chunks)),
-            pltpu.SemaphoreType.DMA((3, chunks)),
-            pltpu.SemaphoreType.DMA((4, 2)),
-            pltpu.SemaphoreType.DMA((4, 2)),
-            pltpu.SemaphoreType.DMA((4, 2)),
-            pltpu.SemaphoreType.DMA((4, 2)),
-            pltpu.SemaphoreType.DMA((4, 2)),
+            pltpu.VMEM((peers,) + codes.shape, bf16),
+            pltpu.VMEM((SCALE_ROWS, HEAD), f32),
+            pltpu.VMEM((peers, SCALE_ROWS, HEAD), f32),
+            pltpu.VMEM((peers + 1,) + codes.shape, bf16),
+            pltpu.VMEM((heads * SPAN, HEAD), bf16),
+            pltpu.VMEM((codes.shape[0], 2 * SPAN, SPAN), f32),
+            pltpu.VMEM((heads * SPAN, HEAD), f32),
+            pltpu.VMEM((heads * SPAN, HEAD), f32),
+            pltpu.VMEM((heads * SPAN, HEAD), f32),
+            pltpu.VMEM((table_rows, SPAN), f32),
+            dma((4,)),
+            dma((peers,)),
+            dma((3, chunks)),
+            dma((3, chunks)),
+            dma((4, 2)),
+            dma((4, 2)),
+            dma((4, 2)),
+            dma((4, 2)),
+            dma((4, 2)),
         ],
         compiler_params=pltpu.CompilerParams(
-            collective_id=0, has_side_effects=True, vmem_limit_bytes=48 * 2**20
+            collective_id=0, has_side_effects=True, vmem_limit_bytes=60 * 2**20
         ),
-        name="gather_project",
-    )(hidden, codes, scales, w_q, w_kv, gain, angles)
+        name="stream_attend",
+    )(home, ids, count, query_len, hidden, codes, scales, w_q, w_kv, gain, recompute,
+      inverse_freq()[None, :], doc_cos, doc_sin)
+
+
+def place_kernel(
+    home, ids, count, recompute, attended, cached, new_k, new_v,
+    out, context,
+    fetched, key_rows, value_rows, keys, values, fetch_sem, out_sem,
+):
+    docs = count[0]
+    passed = pltpu.make_async_copy(attended, out, out_sem.at[2])
+    passed.start()
+
+    def fetch(j):
+        return pltpu.make_async_copy(cached.at[home[ids[0, j]]], fetched.at[j], fetch_sem.at[j])
+
+    lax.fori_loop(0, docs, lambda j, n: (fetch(j).start(), n)[1], 0)
+
+    def widen(j, carry):
+        rows = pl.ds(pl.multiple_of(j * SPAN, SPAN), SPAN)
+
+        @pl.when(j < docs)
+        def _():
+            fetch(j).wait()
+            key_rows[rows, :] = fetched[j, 0].astype(f32)
+            value_rows[rows, :] = fetched[j, 1].astype(f32)
+
+        @pl.when(j >= docs)
+        def _():
+            key_rows[rows, :] = jnp.zeros((SPAN, HEAD), f32)
+            value_rows[rows, :] = jnp.zeros((SPAN, HEAD), f32)
+
+        return carry
+
+    lax.fori_loop(0, MAXDOC, widen, 0)
+    step = 16
+
+    def patch(i, carry):
+        for u in range(step):
+            source = i * step + u
+            row = recompute[source // CHUNK, source % CHUNK]
+            key_rows[pl.ds(row, 1), :] = new_k[pl.ds(source, 1), :]
+            value_rows[pl.ds(row, 1), :] = new_v[pl.ds(source, 1), :]
+        return carry
+
+    lax.fori_loop(0, new_k.shape[0] // step, patch, 0)
+    writes = [
+        pltpu.make_async_copy(keys, context.at[0], out_sem.at[0]),
+        pltpu.make_async_copy(values, context.at[1], out_sem.at[1]),
+    ]
+    for source, target, copy in ((key_rows, keys, writes[0]), (value_rows, values, writes[1])):
+        def narrow(j, carry, source=source, target=target):
+            rows = pl.ds(pl.multiple_of(j * SPAN, SPAN), SPAN)
+            target[rows, :] = source[rows, :].astype(bf16)
+            return carry
+
+        lax.fori_loop(0, MAXDOC, narrow, 0)
+        copy.start()
+    for copy in writes:
+        copy.wait()
+    passed.wait()
+
+
+def place(home, ids, count, recompute, attended, cached, new_k, new_v):
+    context_max = MAXDOC * SPAN
+    return pl.pallas_call(
+        place_kernel,
+        out_shape=(
+            jax.ShapeDtypeStruct(attended.shape, bf16),
+            jax.ShapeDtypeStruct((2, context_max, HEAD), bf16),
+        ),
+        in_specs=[SMEM] * 4 + [ANY, ANY, VMEM, VMEM],
+        out_specs=(ANY, ANY),
+        scratch_shapes=[
+            pltpu.VMEM((MAXDOC, 2, SPAN, HEAD), bf16),
+            pltpu.VMEM((context_max, HEAD), f32),
+            pltpu.VMEM((context_max, HEAD), f32),
+            pltpu.VMEM((context_max, HEAD), bf16),
+            pltpu.VMEM((context_max, HEAD), bf16),
+            pltpu.SemaphoreType.DMA((MAXDOC,)),
+            pltpu.SemaphoreType.DMA((3,)),
+        ],
+        compiler_params=pltpu.CompilerParams(vmem_limit_bytes=60 * 2**20),
+        name="place_context",
+    )(home, ids, count, recompute, attended, cached, new_k, new_v)
 
 
 def plain_gather_and_project(hidden, codes, scales, w_q, w_kv, gain, angles):
@@ -432,17 +684,24 @@
 ):
     peers, tp = lax.axis_size("store"), lax.axis_size("tp")
     stored = kv_store.shape[0]
+    gain = norm_gain.astype(f32).reshape(1, -1)
+    pairs = w_kv.reshape(-1, HEAD)
+    if (peers, tp) == (8, 4):
+        attended, new_k, new_v, cached = stream(
+            peers, tp, span_home, doc_ids, doc_count, query_len, hidden[0], kv_store, kv_scale, w_q, pairs, gain,
+            recompute_rows[0],
+        )
+        cached = cached.reshape((peers * stored,) + kv_store.shape[1:])
+        attention, context = place(
+            span_home, doc_ids, doc_count, recompute_rows[0], attended, cached, new_k, new_v
+        )
+        return attention[None], context[None]
     scales = jnp.broadcast_to(kv_scale.reshape(stored * 4, 1), (stored * 4, HEAD))
     scales = jnp.pad(scales, ((0, SCALE_ROWS - stored * 4), (0, 0)))
     flat = recompute_rows.reshape(-1)
     row_pos = jnp.concatenate([flat, doc_count[0] * SPAN + jnp.arange(SPAN, dtype=jnp.int32)])
     angles = row_pos.astype(f32)[:, None] * inverse_freq()[None, :]
-    gain = norm_gain.astype(f32).reshape(1, -1)
-    pairs = w_kv.reshape(-1, HEAD)
-    if (peers, tp) == (8, 4):
-        gathered = gather_and_project(peers, tp, hidden[0], kv_store, scales, w_q, pairs, gain, angles)
-    else:
-        gathered = plain_gather_and_project(hidden[0], kv_store, scales, w_q, pairs, gain, angles)
+    gathered = plain_gather_and_project(hidden[0], kv_store, scales, w_q, pairs, gain, angles)
     q, new_k, new_v, codes, all_scales = gathered
     attention, context = attend(
         stored, span_home, doc_ids, doc_count, flat, query_len,

time: 75.1 us -> 70.8 us (0.943)
  the two profiles are of different devices: /device:TPU:25 before, /device:TPU:0 now
where the time goes in v2:
time: 70.8 us; the launch traced here: 70.4 us
  Pallas kernels  65.7 us (93%)
  between operations  2.09 us (3%)
  local copies, waits for them, and re-layouts  1.37 us (2%)
  other arithmetic  1.3 us (2%)
    pallas_call x1, Pallas kernels, stream(): pl.pallas_call(stream_kernel, out_shape=(jax.ShapeDtypeStruct((SPAN, head...  55.4 us
    pallas_call x1, Pallas kernels, place(): pl.pallas_call(place_kernel, out_shape=(jax.ShapeDtypeStruct(attended.sha...  10.3 us

profile of v2, /device:TPU:0, one launch (start us, length us, event | category | flops | bytes accessed | tf_op | source)
XLA Modules:
  0.0 70.4 jit_solution(14862557978485594838)
XLA Ops:
  1.9 1.4 %copy.16.scales = bf16[3,2,1,2]{3,2,1,0:T(2,128)(2,1)} copy(bf16[3,2,1,2]{0,3,2,1:T(2,128)(2,1)} %param.15) | data formatting | bytes 48 | tf_op args[1]
  3.3 1.3 %reshape.19 = f32[4096]{0:T(1024)} convert(bf16[4096]{0:T(1024)(128)(2,1)} %param.22) | non-fusion elementwise | flops 4096 | bytes 24576 | tf_op jit(solution)/shard_map/reshape | solution.py:687
  4.6 55.4 %stream_attend.1 = (bf16[256,512]{1,0:T(8,128)(2,1)}, f32[512,128]{1,0:T(8,128)}, f32[512,128]{1,0:T(8,128)}, bf16[8,3,2,256,128]{4,3,2,1,0:T(8,128)(2,1)}) custom-call(s32[24]{0:T(128)} %home.3, s32[1,20]{1,0:T(1,128)} %ids.3, s32[1]{0:T(128)S(6)} %copy.17.count, s32[1]{0:T(128)S(6)} %copy.18.query_len, bf16[768,1024]{1,0:T(8,128)(2,1)} %bitcast.9, ...), custom_call_target="tpu_custom_call" | custom-call | tf_op jit(solution)/shard_map/stream_attend/pallas_call | solution.py:382
  60.0 10.3 %place_context.1 = (bf16[256,512]{1,0:T(8,128)(2,1)}, bf16[2,5120,128]{2,1,0:T(8,128)(2,1)}) custom-call(s32[24]{0:T(128)} %home.3, s32[1,20]{1,0:T(1,128)} %ids.3, s32[1]{0:T(128)S(6)} %copy.17.count, s32[4,128]{1,0:T(4,128)} %bitcast.12, bf16[256,512]{1,0:T(8,128)(2,1)} %get-tuple-element.8.attended, bf16[24,2,256,128]{3,2,1,0:T(8,128)(2,1)} %bitcast.7, ...), custom_call_target="tpu_custom_call" | custom-call | tf_op jit(solution)/shard_map/place_context/pallas_call | solution.py:487

commit v3 on v2

--- a/solution.py
+++ b/solution.py
@@ -19,6 +19,8 @@
 norm_eps = 1e-05
 MASKED = -1e30
 LOG2E = 1.4426950408889634
+NORM_ROWS = 16
+TILE = 32
 f32, bf16 = jnp.float32, jnp.bfloat16
 MESH = pl.DeviceIdType.MESH
 ANY = pl.BlockSpec(memory_space=pl.ANY)
@@ -43,8 +45,9 @@
 
 def stream_kernel(
     home, ids, count, query_len, hidden, codes, scales, w_q, w_kv, gain, recompute, freq, doc_cos, doc_sin,
-    attn_out, k_out, v_out, cached_out,
-    hid, wq, wkv_raw, wkv, wide, codes_all, scales_own, scales_all, cached, queries, scores, top, total, mixed, hidden_rows,
+    attn_out, fresh_out, cached_out,
+    hid, wq, wkv_raw, wkv, wide, codes_all, scales_own, scales_all, cached, queries, scores, weights, normed, gains,
+    top, total, mixed, hidden_rows,
     local_sem, cached_sem, hid_send, hid_recv, up_send, down_send, x_send, z_recv, x_recv,
 ):
     s = lax.axis_index("store")
@@ -84,10 +87,10 @@
     scales_own[...] = jnp.zeros(scales_own.shape, f32)
     for i in range(stored):
         for part in range(2):
-            pair = scales[i, part].astype(f32)
+            pair = scales[0, part].astype(f32)
             for b in range(blocks):
                 row = (i * 2 + part) * blocks + b
-                scales_own[row:row + 1, :] = jnp.broadcast_to(pair[:, b:b + 1], (1, HEAD))
+                scales_own[row:row + 1, :] = jnp.broadcast_to(pair[b:b + 1, i:i + 1], (1, HEAD))
     pl.semaphore_wait(barrier, 3 + jnp.where(z > 0, 1, 0) + jnp.where(z < last, 1, 0))
 
     def span_copies(own, owner_z, column, send, recv, target):
@@ -143,6 +146,7 @@
     for chunk in order:
         hidden_copy(1, chunk).start()
 
+    gains[...] = gain[...].astype(f32).reshape(gains.shape)
     docs = count[0]
     positions = [home[ids[0, j]] for j in range(MAXDOC)]
     table_rows = hidden_rows.shape[0]
@@ -189,77 +193,104 @@
         diagonal_entry = down_rows == lax.broadcasted_iota(jnp.int32, (CHUNK, CHUNK), 1)
         return jnp.sum(jnp.where(diagonal_entry, row, 0.0), axis=1, keepdims=True) * freq[...]
 
-    def project(chunk):
+    def normalise(chunk, place):
         hidden_arrival(1, chunk)
         hidden_arrival(2, chunk)
-        rows = pl.ds(chunk * CHUNK, CHUNK)
-        squares = jnp.zeros((CHUNK, 1), f32)
-        for part in range(parts):
-            values = hid[part, rows, :].astype(f32)
-            squares = squares + jnp.sum(values * values, axis=1, keepdims=True)
-        inverse_rms = lax.rsqrt(squares * (1.0 / (parts * width)) + norm_eps)
-        kv = jnp.zeros((CHUNK, 2 * HEAD), f32)
-        is_query = chunk >= first_query
-        q = jnp.zeros((CHUNK, wq.shape[1]), f32)
-        for part in range(parts):
-            columns = pl.ds(part * width, width)
-            normed = (hid[part, rows, :].astype(f32) * inverse_rms * gain[:, columns]).astype(bf16)
-            kv = kv + jnp.dot(normed, wkv[columns, :], preferred_element_type=f32)
+
+        def some_rows(i, carry):
+            rows = pl.ds(pl.multiple_of(chunk * CHUNK + i * NORM_ROWS, NORM_ROWS), NORM_ROWS)
+            placed = pl.ds(pl.multiple_of(place * CHUNK + i * NORM_ROWS, NORM_ROWS), NORM_ROWS)
+            squares = jnp.zeros((NORM_ROWS, HEAD), f32)
+            for part in range(parts):
+                for block in range(width // HEAD):
+                    value = hid[part, rows, block * HEAD:(block + 1) * HEAD].astype(f32)
+                    squares = squares + value * value
+            mean = jnp.sum(squares, axis=1, keepdims=True) * (1.0 / (parts * width))
+            inverse_rms = jnp.broadcast_to(lax.rsqrt(mean + norm_eps), (NORM_ROWS, HEAD))
+            for part in range(parts):
+                for block in range(width // HEAD):
+                    first = part * width + block * HEAD
+                    value = hid[part, rows, block * HEAD:(block + 1) * HEAD].astype(f32)
+                    value = value * inverse_rms * gains[:, first:first + HEAD]
+                    normed[placed, first:first + HEAD] = value.astype(bf16)
+            return carry
+
+        lax.fori_loop(0, CHUNK // NORM_ROWS, some_rows, 0)
+
+    def project(group):
+        for n, chunk in enumerate(group):
+            normalise(chunk, n)
+        ready = normed[0:len(group) * CHUNK, :]
+        kv_all = jnp.dot(ready, wkv[...], preferred_element_type=f32)
+        is_query = group[0] >= first_query
+        if is_query:
+            q_all = jnp.dot(ready, wq[...], preferred_element_type=f32)
+        per_span = SPAN // CHUNK
+        for n, chunk in enumerate(group):
+            rows = pl.ds(chunk * CHUNK, CHUNK)
+            here = slice(n * CHUNK, (n + 1) * CHUNK)
+            angle = row_angles(chunk)
+            cosine, sine = jnp.cos(angle), jnp.sin(angle)
+            sine = jnp.where(lax.broadcasted_iota(jnp.int32, angle.shape, 1) < HALF, -sine, sine)
+            new_key = rotate(kv_all[here, :HEAD], cosine, sine).astype(bf16)
+            new_value = kv_all[here, HEAD:].astype(bf16)
+            place = pl.ds(chunk % per_span * CHUNK, CHUNK)
+            cached[own_slot, chunk // per_span, 0, place, :] = new_key
+            cached[own_slot, chunk // per_span, 1, place, :] = new_value
             if is_query:
-                q = q + jnp.dot(normed, wq[columns, :], preferred_element_type=f32)
-        angle = row_angles(chunk)
-        cosine, sine = jnp.cos(angle), jnp.sin(angle)
-        sine = jnp.where(lax.broadcasted_iota(jnp.int32, angle.shape, 1) < HALF, -sine, sine)
-        new_key = rotate(kv[:, :HEAD], cosine, sine)
-        per_span = SPAN // CHUNK
-        place = pl.ds(chunk % per_span * CHUNK, CHUNK)
-        cached[own_slot, chunk // per_span, 0, place, :] = new_key.astype(bf16)
-        cached[own_slot, chunk // per_span, 1, place, :] = kv[:, HEAD:].astype(bf16)
-        if is_query:
-            for g in range(heads):
-                q_rows = pl.ds(g * SPAN + (chunk - first_query) * CHUNK, CHUNK)
-                queries[q_rows, :] = rotate(q[:, g * HEAD:(g + 1) * HEAD], cosine, sine).astype(bf16)
-        else:
-            k_out[rows, :] = new_key
-            v_out[rows, :] = kv[:, HEAD:]
+                for g in range(heads):
+                    q_rows = pl.ds(g * SPAN + (chunk - first_query) * CHUNK, CHUNK)
+                    q = q_all[here, g * HEAD:(g + 1) * HEAD]
+                    queries[q_rows, :] = rotate(q, cosine, sine).astype(bf16)
+            else:
+                fresh_out[rows, :HEAD] = new_key
+                fresh_out[rows, HEAD:] = new_value
 
     exponent = HEAD ** (-0.5) * LOG2E
-    query_block = scores.shape[1]
+    halves, _, query_block, _ = scores.shape
 
     def attend_group(slot, bias, causal):
-        def some_queries(n, carry):
-            rows = pl.ds(pl.multiple_of(n * query_block, query_block), query_block)
-            q = queries[rows, :]
-            before = top[rows, :]
-            peak = before
+        for n in range(halves):
+            q = queries[n * query_block:(n + 1) * query_block, :]
             for i in range(stored):
-                part = lax.dot_general(
+                scores[n, i] = lax.dot_general(
                     q, cached[slot, i, 0], (((1,), (1,)), ((), ())), preferred_element_type=f32
                 )
-                if bias is not None:
-                    part = part + bias[i]
-                elif causal and i == stored - 1:
-                    query_index = lax.broadcasted_iota(jnp.int32, (query_block, SPAN), 0) & (SPAN - 1)
-                    key_index = lax.broadcasted_iota(jnp.int32, (query_block, SPAN), 1)
-                    part = jnp.where(key_index <= query_index, part, MASKED)
-                scores[i] = part
-                peak = jnp.maximum(peak, jnp.maximum(part[:, :HEAD], part[:, HEAD:]))
-            peak = jnp.broadcast_to(jnp.max(peak, axis=1, keepdims=True), (query_block, HEAD))
-            top[rows, :] = peak
-            fade = jnp.exp2((before - peak) * exponent)
-            sums = total[rows, :] * fade
-            gained = jnp.zeros((query_block, HEAD), f32)
-            for i in range(stored):
-                low = jnp.exp2((scores[i, :, :HEAD] - peak) * exponent)
-                high = jnp.exp2((scores[i, :, HEAD:] - peak) * exponent)
-                sums = sums + (low + high)
-                weights = jnp.concatenate([low.astype(bf16), high.astype(bf16)], axis=1)
-                gained = gained + jnp.dot(weights, cached[slot, i, 1], preferred_element_type=f32)
-            total[rows, :] = sums
-            mixed[rows, :] = mixed[rows, :] * fade + gained
-            return carry
-
-        lax.fori_loop(0, queries.shape[0] // query_block, some_queries, 0)
+        for n in range(halves):
+            for tile in range(query_block // TILE):
+                here = slice(tile * TILE, (tile + 1) * TILE)
+                rows = slice(n * query_block + tile * TILE, n * query_block + (tile + 1) * TILE)
+
+                def part(i, side):
+                    value = scores[n, i, here, side * HEAD:(side + 1) * HEAD]
+                    if bias is not None:
+                        return value + bias[i][:, side * HEAD:(side + 1) * HEAD]
+                    if causal and i == stored - 1:
+                        query_index = lax.broadcasted_iota(jnp.int32, (TILE, HEAD), 0) + tile * TILE % SPAN
+                        key_index = lax.broadcasted_iota(jnp.int32, (TILE, HEAD), 1) + side * HEAD
+                        return jnp.where(key_index <= query_index, value, MASKED)
+                    return value
+
+                before = top[rows, :]
+                peak = before
+                for i in range(stored):
+                    peak = jnp.maximum(peak, jnp.maximum(part(i, 0), part(i, 1)))
+                peak = jnp.broadcast_to(jnp.max(peak, axis=1, keepdims=True), (TILE, HEAD))
+                top[rows, :] = peak
+                fade = jnp.exp2((before - peak) * exponent)
+                sums = total[rows, :] * fade
+                for i in range(stored):
+                    for side in range(2):
+                        weight = jnp.exp2((part(i, side) - peak) * exponent)
+                        sums = sums + weight
+                        weights[n, i, here, side * HEAD:(side + 1) * HEAD] = weight.astype(bf16)
+                total[rows, :] = sums
+                mixed[rows, :] = mixed[rows, :] * fade
+            rows = slice(n * query_block, (n + 1) * query_block)
+            gained = jnp.dot(weights[n, 0], cached[slot, 0, 1], preferred_element_type=f32)
+            for i in range(1, stored):
+                gained = gained + jnp.dot(weights[n, i], cached[slot, i, 1], preferred_element_type=f32)
+            mixed[rows, :] += gained
 
     def keep_cached(slot):
         return pltpu.make_async_copy(cached.at[slot], cached_out.at[slot], cached_sem.at[slot])
@@ -318,29 +349,26 @@
         hidden_arrival(0, order[i])
         hidden_copy(2, order[i]).start()
 
+    scales_all[s] = scales_own[...]
     relay(0)
-    scales_all[s] = scales_own[...]
-    project(order[0])
     span_step(1)
     relay(1)
-    project(order[1])
+    project(order[0:2])
     same_column(0)
     relay(2)
     span_step(2)
     other_column(0)
-    project(order[2])
     same_column(1)
     relay(3)
     span_step(3)
+    project(order[2:4])
     other_column(1)
-    project(order[3])
     relay(4)
     same_column(2)
     same_column(3)
-    project(order[4])
+    relay(5)
+    project(order[4:6])
     other_column(2)
-    relay(5)
-    project(order[5])
     attend_group(own_slot, None, True)
     other_column(3)
 
@@ -383,12 +411,11 @@
         stream_kernel,
         out_shape=(
             jax.ShapeDtypeStruct((SPAN, heads * HEAD), bf16),
-            jax.ShapeDtypeStruct((fresh, HEAD), f32),
-            jax.ShapeDtypeStruct((fresh, HEAD), f32),
+            jax.ShapeDtypeStruct((fresh, 2 * HEAD), bf16),
             jax.ShapeDtypeStruct((peers,) + codes.shape, bf16),
         ),
         in_specs=[SMEM] * 4 + [ANY, ANY, VMEM, ANY, ANY] + [VMEM] * 5,
-        out_specs=(VMEM, VMEM, VMEM, ANY),
+        out_specs=(VMEM, VMEM, ANY),
         scratch_shapes=[
             pltpu.VMEM((tp, rows, width), bf16),
             pltpu.VMEM((features, w_q.shape[1]), bf16),
@@ -400,7 +427,10 @@
             pltpu.VMEM((peers, SCALE_ROWS, HEAD), f32),
             pltpu.VMEM((peers + 1,) + codes.shape, bf16),
             pltpu.VMEM((heads * SPAN, HEAD), bf16),
-            pltpu.VMEM((codes.shape[0], 2 * SPAN, SPAN), f32),
+            pltpu.VMEM((heads // 2, codes.shape[0], 2 * SPAN, SPAN), f32),
+            pltpu.VMEM((heads // 2, codes.shape[0], 2 * SPAN, SPAN), bf16),
+            pltpu.VMEM((SPAN, features), bf16),
+            pltpu.VMEM((1, features), f32),
             pltpu.VMEM((heads * SPAN, HEAD), f32),
             pltpu.VMEM((heads * SPAN, HEAD), f32),
             pltpu.VMEM((heads * SPAN, HEAD), f32),
@@ -424,65 +454,62 @@
 
 
 def place_kernel(
-    home, ids, count, recompute, attended, cached, new_k, new_v,
+    home, ids, count, recompute, attended, cached, fresh,
     out, context,
-    fetched, key_rows, value_rows, keys, values, fetch_sem, out_sem,
+    fetched, placed, fetch_sem, write_sem, out_sem,
 ):
     docs = count[0]
-    passed = pltpu.make_async_copy(attended, out, out_sem.at[2])
+    passed = pltpu.make_async_copy(attended, out, out_sem)
     passed.start()
 
     def fetch(j):
         return pltpu.make_async_copy(cached.at[home[ids[0, j]]], fetched.at[j], fetch_sem.at[j])
 
+    def write(j, part):
+        rows = pl.ds(pl.multiple_of(j * SPAN, SPAN), SPAN)
+        return pltpu.make_async_copy(placed.at[j, part], context.at[part, rows], write_sem.at[j, part])
+
     lax.fori_loop(0, docs, lambda j, n: (fetch(j).start(), n)[1], 0)
-
-    def widen(j, carry):
-        rows = pl.ds(pl.multiple_of(j * SPAN, SPAN), SPAN)
-
+    ones = jnp.ones((fresh.shape[0], HEAD), bf16)
+
+    def fill(j, carry):
         @pl.when(j < docs)
         def _():
+            rows = lax.broadcasted_iota(jnp.int32, (SPAN, CHUNK), 0) + j * SPAN
+            match = jnp.concatenate(
+                [
+                    jnp.where(recompute[r:r + 1, :] == rows, 1.0, 0.0).astype(bf16)
+                    for r in range(recompute.shape[0])
+                ],
+                axis=1,
+            )
+            hit = jnp.dot(match, ones, preferred_element_type=f32) > 0.5
+            patch = jnp.dot(match, fresh[...], preferred_element_type=f32)
             fetch(j).wait()
-            key_rows[rows, :] = fetched[j, 0].astype(f32)
-            value_rows[rows, :] = fetched[j, 1].astype(f32)
+            for part in range(2):
+                new = patch[:, part * HEAD:(part + 1) * HEAD]
+                placed[j, part] = jnp.where(hit, new, fetched[j, part].astype(f32)).astype(bf16)
 
         @pl.when(j >= docs)
         def _():
-            key_rows[rows, :] = jnp.zeros((SPAN, HEAD), f32)
-            value_rows[rows, :] = jnp.zeros((SPAN, HEAD), f32)
-
+            placed[j] = jnp.zeros(placed.shape[1:], bf16)
+
+        write(j, 0).start()
+        write(j, 1).start()
         return carry
 
-    lax.fori_loop(0, MAXDOC, widen, 0)
-    step = 16
-
-    def patch(i, carry):
-        for u in range(step):
-            source = i * step + u
-            row = recompute[source // CHUNK, source % CHUNK]
-            key_rows[pl.ds(row, 1), :] = new_k[pl.ds(source, 1), :]
-            value_rows[pl.ds(row, 1), :] = new_v[pl.ds(source, 1), :]
+    lax.fori_loop(0, MAXDOC, fill, 0)
+
+    def drain(j, carry):
+        write(j, 0).wait()
+        write(j, 1).wait()
         return carry
 
-    lax.fori_loop(0, new_k.shape[0] // step, patch, 0)
-    writes = [
-        pltpu.make_async_copy(keys, context.at[0], out_sem.at[0]),
-        pltpu.make_async_copy(values, context.at[1], out_sem.at[1]),
-    ]
-    for source, target, copy in ((key_rows, keys, writes[0]), (value_rows, values, writes[1])):
-        def narrow(j, carry, source=source, target=target):
-            rows = pl.ds(pl.multiple_of(j * SPAN, SPAN), SPAN)
-            target[rows, :] = source[rows, :].astype(bf16)
-            return carry
-
-        lax.fori_loop(0, MAXDOC, narrow, 0)
-        copy.start()
-    for copy in writes:
-        copy.wait()
+    lax.fori_loop(0, MAXDOC, drain, 0)
     passed.wait()
 
 
-def place(home, ids, count, recompute, attended, cached, new_k, new_v):
+def place(home, ids, count, recompute, attended, cached, fresh):
     context_max = MAXDOC * SPAN
     return pl.pallas_call(
         place_kernel,
@@ -490,20 +517,18 @@
             jax.ShapeDtypeStruct(attended.shape, bf16),
             jax.ShapeDtypeStruct((2, context_max, HEAD), bf16),
         ),
-        in_specs=[SMEM] * 4 + [ANY, ANY, VMEM, VMEM],
+        in_specs=[SMEM] * 3 + [VMEM, ANY, ANY, VMEM],
         out_specs=(ANY, ANY),
         scratch_shapes=[
             pltpu.VMEM((MAXDOC, 2, SPAN, HEAD), bf16),
-            pltpu.VMEM((context_max, HEAD), f32),
-            pltpu.VMEM((context_max, HEAD), f32),
-            pltpu.VMEM((context_max, HEAD), bf16),
-            pltpu.VMEM((context_max, HEAD), bf16),
+            pltpu.VMEM((MAXDOC, 2, SPAN, HEAD), bf16),
             pltpu.SemaphoreType.DMA((MAXDOC,)),
-            pltpu.SemaphoreType.DMA((3,)),
+            pltpu.SemaphoreType.DMA((MAXDOC, 2)),
+            pltpu.SemaphoreType.DMA,
         ],
         compiler_params=pltpu.CompilerParams(vmem_limit_bytes=60 * 2**20),
         name="place_context",
-    )(home, ids, count, recompute, attended, cached, new_k, new_v)
+    )(home, ids, count, recompute, attended, cached, fresh)
 
 
 def plain_gather_and_project(hidden, codes, scales, w_q, w_kv, gain, angles):
@@ -687,13 +712,13 @@
     gain = norm_gain.astype(f32).reshape(1, -1)
     pairs = w_kv.reshape(-1, HEAD)
     if (peers, tp) == (8, 4):
-        attended, new_k, new_v, cached = stream(
-            peers, tp, span_home, doc_ids, doc_count, query_len, hidden[0], kv_store, kv_scale, w_q, pairs, gain,
-            recompute_rows[0],
+        attended, fresh, cached = stream(
+            peers, tp, span_home, doc_ids, doc_count, query_len, hidden[0], kv_store,
+            jnp.transpose(kv_scale, (2, 1, 3, 0)), w_q, pairs, norm_gain, recompute_rows[0],
         )
         cached = cached.reshape((peers * stored,) + kv_store.shape[1:])
         attention, context = place(
-            span_home, doc_ids, doc_count, recompute_rows[0], attended, cached, new_k, new_v
+            span_home, doc_ids, doc_count, recompute_rows[0], attended, cached, fresh
         )
         return attention[None], context[None]
     scales = jnp.broadcast_to(kv_scale.reshape(stored * 4, 1), (stored * 4, HEAD))

time: 70.8 us -> 70.2 us (level)
  Pallas kernels: 65.7 us -> 67.8 us
  local copies, waits for them, and re-layouts: 1.37 us -> 0 us
  other arithmetic: 1.3 us -> 0 us
    pallas_call x1, Pallas kernels: 55.4 us -> 57.3 us  [stream(): pl.pallas_call(stream_kernel, out_shape=(jax.ShapeDtypeStruct((SPAN, head...]
    unnamed x1 -> x0, local copies, waits for them, and re-layouts: 1.37 us -> none
    reshape x1 -> x0, other arithmetic: 1.3 us -> none  [on_device(): gain = norm_gain.astype(f32).reshape(1, -1)]
where the time goes in v3:
time: 70.2 us; the launch traced here: 69.9 us
  Pallas kernels  67.8 us (97%)
  between operations  2.11 us (3%)
    pallas_call x1, Pallas kernels, stream(): pl.pallas_call(stream_kernel, out_shape=(jax.ShapeDtypeStruct((SPAN, head...  57.3 us
    pallas_call x1, Pallas kernels, place(): pl.pallas_call(place_kernel, out_shape=(jax.ShapeDtypeStruct(attended.sha...  10.6 us

profile of v3, /device:TPU:0, one launch (start us, length us, event | category | flops | bytes accessed | tf_op | source)
XLA Modules:
  0.0 69.9 jit_solution(6673806907510323951)
XLA Ops:
  1.9 57.3 %stream_attend.1 = (bf16[256,512]{1,0:T(8,128)(2,1)}, bf16[512,256]{1,0:T(8,128)(2,1)}, bf16[8,3,2,256,128]{4,3,2,1,0:T(8,128)(2,1)}) custom-call(s32[24]{0:T(128)} %home.3, s32[1,20]{1,0:T(1,128)} %ids.3, s32[1]{0:T(128)S(6)} %copy.17.count, s32[1]{0:T(128)S(6)} %copy.18.query_len, bf16[768,1024]{1,0:T(8,128)(2,1)} %bitcast.11, ...), custom_call_target="tpu_custom_call" | custom-call | tf_op jit(solution)/shard_map/stream_attend/pallas_call | solution.py:410
  59.2 10.6 %place_context.1 = (bf16[256,512]{1,0:T(8,128)(2,1)}, bf16[2,5120,128]{2,1,0:T(8,128)(2,1)}) custom-call(s32[24]{0:T(128)} %home.3, s32[1,20]{1,0:T(1,128)} %ids.3, s32[1]{0:T(128)S(6)} %copy.17.count, s32[4,128]{1,0:T(4,128)} %bitcast.13, bf16[256,512]{1,0:T(8,128)(2,1)} %get-tuple-element.7.attended, bf16[24,2,256,128]{3,2,1,0:T(8,128)(2,1)} %bitcast.9, ...), custom_call_target="tpu_custom_call" | custom-call | tf_op jit(solution)/shard_map/place_context/pallas_call | solution.py:514

commit v4 on v3

--- a/solution.py
+++ b/solution.py
@@ -20,7 +20,6 @@
 MASKED = -1e30
 LOG2E = 1.4426950408889634
 NORM_ROWS = 16
-TILE = 32
 f32, bf16 = jnp.float32, jnp.bfloat16
 MESH = pl.DeviceIdType.MESH
 ANY = pl.BlockSpec(memory_space=pl.ANY)
@@ -46,7 +45,7 @@
 def stream_kernel(
     home, ids, count, query_len, hidden, codes, scales, w_q, w_kv, gain, recompute, freq, doc_cos, doc_sin,
     attn_out, fresh_out, cached_out,
-    hid, wq, wkv_raw, wkv, wide, codes_all, scales_own, scales_all, cached, queries, scores, weights, normed, gains,
+    hid, wq, wkv_raw, wkv, wide, codes_all, scales_own, scales_all, cached, queries, scores, normed, gains,
     top, total, mixed, hidden_rows,
     local_sem, cached_sem, hid_send, hid_recv, up_send, down_send, x_send, z_recv, x_recv,
 ):
@@ -247,50 +246,42 @@
                 fresh_out[rows, HEAD:] = new_value
 
     exponent = HEAD ** (-0.5) * LOG2E
-    halves, _, query_block, _ = scores.shape
+    query_block = scores.shape[1]
 
     def attend_group(slot, bias, causal):
-        for n in range(halves):
-            q = queries[n * query_block:(n + 1) * query_block, :]
+        def some_queries(n, carry):
+            rows = pl.ds(pl.multiple_of(n * query_block, query_block), query_block)
+            q = queries[rows, :]
+            before = top[rows, :]
+            peak = before
             for i in range(stored):
-                scores[n, i] = lax.dot_general(
+                part = lax.dot_general(
                     q, cached[slot, i, 0], (((1,), (1,)), ((), ())), preferred_element_type=f32
                 )
-        for n in range(halves):
-            for tile in range(query_block // TILE):
-                here = slice(tile * TILE, (tile + 1) * TILE)
-                rows = slice(n * query_block + tile * TILE, n * query_block + (tile + 1) * TILE)
-
-                def part(i, side):
-                    value = scores[n, i, here, side * HEAD:(side + 1) * HEAD]
-                    if bias is not None:
-                        return value + bias[i][:, side * HEAD:(side + 1) * HEAD]
-                    if causal and i == stored - 1:
-                        query_index = lax.broadcasted_iota(jnp.int32, (TILE, HEAD), 0) + tile * TILE % SPAN
-                        key_index = lax.broadcasted_iota(jnp.int32, (TILE, HEAD), 1) + side * HEAD
-                        return jnp.where(key_index <= query_index, value, MASKED)
-                    return value
-
-                before = top[rows, :]
-                peak = before
-                for i in range(stored):
-                    peak = jnp.maximum(peak, jnp.maximum(part(i, 0), part(i, 1)))
-                peak = jnp.broadcast_to(jnp.max(peak, axis=1, keepdims=True), (TILE, HEAD))
-                top[rows, :] = peak
-                fade = jnp.exp2((before - peak) * exponent)
-                sums = total[rows, :] * fade
-                for i in range(stored):
-                    for side in range(2):
-                        weight = jnp.exp2((part(i, side) - peak) * exponent)
-                        sums = sums + weight
-                        weights[n, i, here, side * HEAD:(side + 1) * HEAD] = weight.astype(bf16)
-                total[rows, :] = sums
-                mixed[rows, :] = mixed[rows, :] * fade
-            rows = slice(n * query_block, (n + 1) * query_block)
-            gained = jnp.dot(weights[n, 0], cached[slot, 0, 1], preferred_element_type=f32)
-            for i in range(1, stored):
-                gained = gained + jnp.dot(weights[n, i], cached[slot, i, 1], preferred_element_type=f32)
-            mixed[rows, :] += gained
+                if bias is not None:
+                    part = part + bias[i]
+                elif causal and i == stored - 1:
+                    query_index = lax.broadcasted_iota(jnp.int32, (query_block, SPAN), 0) & (SPAN - 1)
+                    key_index = lax.broadcasted_iota(jnp.int32, (query_block, SPAN), 1)
+                    part = jnp.where(key_index <= query_index, part, MASKED)
+                scores[i] = part
+                peak = jnp.maximum(peak, jnp.maximum(part[:, :HEAD], part[:, HEAD:]))
+            peak = jnp.broadcast_to(jnp.max(peak, axis=1, keepdims=True), (query_block, HEAD))
+            top[rows, :] = peak
+            fade = jnp.exp2((before - peak) * exponent)
+            sums = total[rows, :] * fade
+            gained = jnp.zeros((query_block, HEAD), f32)
+            for i in range(stored):
+                low = jnp.exp2((scores[i, :, :HEAD] - peak) * exponent)
+                high = jnp.exp2((scores[i, :, HEAD:] - peak) * exponent)
+                sums = sums + (low + high)
+                weights = jnp.concatenate([low.astype(bf16), high.astype(bf16)], axis=1)
+                gained = gained + jnp.dot(weights, cached[slot, i, 1], preferred_element_type=f32)
+            total[rows, :] = sums
+            mixed[rows, :] = mixed[rows, :] * fade + gained
+            return carry
+
+        lax.fori_loop(0, queries.shape[0] // query_block, some_queries, 0)
 
     def keep_cached(slot):
         return pltpu.make_async_copy(cached.at[slot], cached_out.at[slot], cached_sem.at[slot])
@@ -427,8 +418,7 @@
             pltpu.VMEM((peers, SCALE_ROWS, HEAD), f32),
             pltpu.VMEM((peers + 1,) + codes.shape, bf16),
             pltpu.VMEM((heads * SPAN, HEAD), bf16),
-            pltpu.VMEM((heads // 2, codes.shape[0], 2 * SPAN, SPAN), f32),
-            pltpu.VMEM((heads // 2, codes.shape[0], 2 * SPAN, SPAN), bf16),
+            pltpu.VMEM((codes.shape[0], 2 * SPAN, SPAN), f32),
             pltpu.VMEM((SPAN, features), bf16),
             pltpu.VMEM((1, features), f32),
             pltpu.VMEM((heads * SPAN, HEAD), f32),
@@ -456,11 +446,9 @@
 def place_kernel(
     home, ids, count, recompute, attended, cached, fresh,
     out, context,
-    fetched, placed, fetch_sem, write_sem, out_sem,
+    fetched, placed, fetch_sem, write_sem,
 ):
     docs = count[0]
-    passed = pltpu.make_async_copy(attended, out, out_sem)
-    passed.start()
 
     def fetch(j):
         return pltpu.make_async_copy(cached.at[home[ids[0, j]]], fetched.at[j], fetch_sem.at[j])
@@ -470,6 +458,7 @@
         return pltpu.make_async_copy(placed.at[j, part], context.at[part, rows], write_sem.at[j, part])
 
     lax.fori_loop(0, docs, lambda j, n: (fetch(j).start(), n)[1], 0)
+    out[...] = attended[...]
     ones = jnp.ones((fresh.shape[0], HEAD), bf16)
 
     def fill(j, carry):
@@ -506,7 +495,6 @@
         return carry
 
     lax.fori_loop(0, MAXDOC, drain, 0)
-    passed.wait()
 
 
 def place(home, ids, count, recompute, attended, cached, fresh):
@@ -517,14 +505,13 @@
             jax.ShapeDtypeStruct(attended.shape, bf16),
             jax.ShapeDtypeStruct((2, context_max, HEAD), bf16),
         ),
-        in_specs=[SMEM] * 3 + [VMEM, ANY, ANY, VMEM],
-        out_specs=(ANY, ANY),
+        in_specs=[SMEM] * 3 + [VMEM, VMEM, ANY, VMEM],
+        out_specs=(VMEM, ANY),
         scratch_shapes=[
             pltpu.VMEM((MAXDOC, 2, SPAN, HEAD), bf16),
             pltpu.VMEM((MAXDOC, 2, SPAN, HEAD), bf16),
             pltpu.SemaphoreType.DMA((MAXDOC,)),
             pltpu.SemaphoreType.DMA((MAXDOC, 2)),
-            pltpu.SemaphoreType.DMA,
         ],
         compiler_params=pltpu.CompilerParams(vmem_limit_bytes=60 * 2**20),
         name="place_context",

time: 70.2 us -> 66.7 us (0.950)
  Pallas kernels: 67.8 us -> 63.8 us
    pallas_call x1, Pallas kernels: 10.6 us -> 6.69 us  [place(): pl.pallas_call(place_kernel, out_shape=(jax.ShapeDtypeStruct(attended.sha...]
where the time goes in v4:
time: 66.7 us; the launch traced here: 65.9 us
  Pallas kernels  63.8 us (96%)
  between operations  2.09 us (3%)
    pallas_call x1, Pallas kernels, stream(): pl.pallas_call(stream_kernel, out_shape=(jax.ShapeDtypeStruct((SPAN, head...  57.1 us
    pallas_call x1, Pallas kernels, place(): pl.pallas_call(place_kernel, out_shape=(jax.ShapeDtypeStruct(attended.sha...  6.69 us

profile of v4, /device:TPU:0, one launch (start us, length us, event | category | flops | bytes accessed | tf_op | source)
XLA Modules:
  0.0 65.9 jit_solution(9745202172966287726)
XLA Ops:
  1.9 57.1 %stream_attend.1 = (bf16[256,512]{1,0:T(8,128)(2,1)}, bf16[512,256]{1,0:T(8,128)(2,1)}, bf16[8,3,2,256,128]{4,3,2,1,0:T(8,128)(2,1)}) custom-call(s32[24]{0:T(128)} %home.3, s32[1,20]{1,0:T(1,128)} %ids.3, s32[1]{0:T(128)S(6)} %copy.17.count, s32[1]{0:T(128)S(6)} %copy.18.query_len, bf16[768,1024]{1,0:T(8,128)(2,1)} %bitcast.11, ...), custom_call_target="tpu_custom_call" | custom-call | tf_op jit(solution)/shard_map/stream_attend/pallas_call | solution.py:401
  59.0 6.7 %place_context.1 = (bf16[256,512]{1,0:T(8,128)(2,1)}, bf16[2,5120,128]{2,1,0:T(8,128)(2,1)}) custom-call(s32[24]{0:T(128)} %home.3, s32[1,20]{1,0:T(1,128)} %ids.3, s32[1]{0:T(128)S(6)} %copy.17.count, s32[4,128]{1,0:T(4,128)} %bitcast.13, bf16[256,512]{1,0:T(8,128)(2,1)} %get-tuple-element.7.attended, bf16[24,2,256,128]{3,2,1,0:T(8,128)(2,1)} %bitcast.9, ...), custom_call_target="tpu_custom_call" | custom-call | tf_op jit(solution)/shard_map/place_context/pallas_call | solution.py:502
